TPU v7x, 32 devices: a whole 2x2x4 slice. The times are simulated.
32 devices in a mesh: dp: 16 (over z, x, core), fsdp: 2 (over y).
Axes of the slice: x: 2, y: 2, z: 4, core: 2. Of those that a mesh axis runs over, the one named last changes fastest.
Arguments:
- latents: bfloat16 [32, 256, 1024], P(('dp', 'fsdp')), may hold values from -6 to 6
- pixels: bfloat16 [32, 128, 1024], P(('dp', 'fsdp')), may hold values from -6 to 6
- visible: int32 [32], P(('dp', 'fsdp')), may hold values from 32 to 128, as said below
- out_grad: bfloat16 [32, 256, 1024], P(('dp', 'fsdp')), may hold values from -6 to 6
- panel: float32 [1024, 12288], P(('dp', 'fsdp')), may hold values from -0.75 to 0.75
- panel_moment: float32 [1024, 12288], P(('dp', 'fsdp')), may hold values from -0.625 to 0.625
- panel_square: float32 [1024, 12288], P(('dp', 'fsdp')), may hold values from 0.0004096 to 0.0065536
- down: float32 [4096, 1024], P(('dp', 'fsdp')), may hold values from -0.09375 to 0.09375
- down_moment: float32 [4096, 1024], P(('dp', 'fsdp')), may hold values from -0.625 to 0.625
- down_square: float32 [4096, 1024], P(('dp', 'fsdp')), may hold values from 0.0004096 to 0.0065536
- vectors: float32 [13312], P(('dp', 'fsdp')), may hold values from -1.2 to 4
- vector_moment: float32 [13312], P(('dp', 'fsdp')), may hold values from -1.75 to 1.75
- vector_square: float32 [13312], P(('dp', 'fsdp')), may hold values from 0.0036864 to 0.0589824
Outputs:
- latents_out: bfloat16 [32, 256, 1024], P(('dp', 'fsdp'))
- latents_grad: float32 [32, 256, 1024], P(('dp', 'fsdp'))
- grad_norm: float32 [], replicated
- panel_after: float32 [1024, 12288], P(('dp', 'fsdp'))
- panel_moment_after: float32 [1024, 12288], P(('dp', 'fsdp'))
- panel_square_after: float32 [1024, 12288], P(('dp', 'fsdp'))
- down_after: float32 [4096, 1024], P(('dp', 'fsdp'))
- down_moment_after: float32 [4096, 1024], P(('dp', 'fsdp'))
- down_square_after: float32 [4096, 1024], P(('dp', 'fsdp'))
- vectors_after: float32 [13312], P(('dp', 'fsdp'))
- vector_moment_after: float32 [13312], P(('dp', 'fsdp'))
- vector_square_after: float32 [13312], P(('dp', 'fsdp'))
Inputs may be any that keep to these rules, and one draw needn't show every extreme that they name: Rows of an image at or after its count are padding; some image has all 128 rows visible.
All inputs are finite; a program needn't handle non-finite values.
Results may differ from a plain program's by a relative error of at most 0.015.
Values may be sent and summed in bfloat16 or wider, within the bound.
A program may use at most 320 MiB of HBM per device.

v0:
```python
import jax
import jax.numpy as jnp
from jax import lax
from jax.sharding import PartitionSpec as P

HEADS = 8
STEP = 10


norm_eps = 1e-05
beta_first = 0.9
beta_second = 0.999
adam_eps = 1e-08
rate_matrix = 0.05
rate_vector = 0.5
weight_decay = 0.1
clip_coeff = 0.01
masked_fill = -1e30


def matmul_low(left, right):
    return jnp.dot(left, right, preferred_element_type=jnp.float32)


def rows_inner(left, right):
    return lax.dot_general(
        left, right, (((0,), (0,)), ((), ())), preferred_element_type=jnp.float32
    )


def times_transposed(left, right):
    return lax.dot_general(
        left, right, (((1,), (1,)), ((), ())), preferred_element_type=jnp.float32
    )


def gelu_exact(values):
    return jax.nn.gelu(values, approximate=False)


def norm_forward(values, gain_row, shift_row):
    centre = values - jnp.mean(values, axis=-1, keepdims=True)
    inverse = lax.rsqrt(jnp.mean(centre * centre, axis=-1, keepdims=True) + norm_eps)
    normed = centre * inverse
    return (normed * gain_row + shift_row, normed, inverse)


def norm_backward(grad_out, normed, inverse, gain_row):
    grad_normed = grad_out * gain_row
    grad_values = inverse * (
        grad_normed
        - jnp.mean(grad_normed, axis=-1, keepdims=True)
        - normed * jnp.mean(grad_normed * normed, axis=-1, keepdims=True)
    )
    return (grad_values, jnp.sum(grad_out * normed, axis=0), jnp.sum(grad_out, axis=0))


def to_heads(rows, images, head_count):
    return rows.reshape(images, -1, head_count, rows.shape[1] // head_count)


def masked_scores(queries, key_rows, visible_mask):
    score_scale = queries.shape[-1] ** (-0.5)
    scores = (
        jnp.einsum("bqhd,bkhd->bhqk", queries, key_rows, preferred_element_type=jnp.float32)
        * score_scale
    )
    if visible_mask is not None:
        scores = jnp.where(visible_mask[:, None, None, :], scores, masked_fill)
    return scores


def attend_forward(queries, key_rows, value_rows, visible_mask):
    scores = masked_scores(queries, key_rows, visible_mask)
    row_top = jnp.max(scores, axis=-1, keepdims=True)
    powers = jnp.exp(scores - row_top)
    row_total = jnp.sum(powers, axis=-1, keepdims=True)
    probability = (powers / row_total).astype(jnp.bfloat16)
    mixture = jnp.einsum(
        "bhqk,bkhd->bqhd", probability, value_rows, preferred_element_type=jnp.float32
    )
    return (mixture.astype(jnp.bfloat16), row_top, row_total)


def attend_backward(grad_mix, queries, key_rows, value_rows, visible_mask, row_top, row_total):
    score_scale = queries.shape[-1] ** (-0.5)
    scores = masked_scores(queries, key_rows, visible_mask)
    probability = jnp.exp(scores - row_top) / row_total
    grad_prob = jnp.einsum(
        "bqhd,bkhd->bhqk", grad_mix, value_rows, preferred_element_type=jnp.float32
    )
    inner_sum = jnp.sum(grad_prob * probability, axis=-1, keepdims=True)
    grad_scores = (probability * (grad_prob - inner_sum)).astype(jnp.bfloat16)
    grad_queries = (
        jnp.einsum("bhqk,bkhd->bqhd", grad_scores, key_rows, preferred_element_type=jnp.float32)
        * score_scale
    )
    grad_keys = (
        jnp.einsum("bhqk,bqhd->bkhd", grad_scores, queries, preferred_element_type=jnp.float32)
        * score_scale
    )
    grad_values = jnp.einsum(
        "bhqk,bqhd->bkhd",
        probability.astype(jnp.bfloat16),
        grad_mix,
        preferred_element_type=jnp.float32,
    )
    return (grad_queries, grad_keys, grad_values)


def vector_slot(vector_float, index, model_width):
    return vector_float[index * model_width : (index + 1) * model_width]


def self_forward(first_sum, self_columns, gain_self, shift_self, images):
    model_width = first_sum.shape[1]
    normed_out, normed, inverse = norm_forward(first_sum, gain_self, shift_self)
    self_low = normed_out.astype(jnp.bfloat16)
    triple = matmul_low(self_low, self_columns[:, : 3 * model_width]).astype(jnp.bfloat16)
    self_queries = to_heads(triple[:, :model_width], images, HEADS)
    self_keys = to_heads(triple[:, model_width : 2 * model_width], images, HEADS)
    self_values = to_heads(triple[:, 2 * model_width :], images, HEADS)
    mixture, row_top, row_total = attend_forward(self_queries, self_keys, self_values, None)
    self_mixed = mixture.reshape(-1, model_width)
    return (
        normed,
        inverse,
        self_low,
        self_queries,
        self_keys,
        self_values,
        self_mixed,
        row_top,
        row_total,
    )


def adam_update(weight, moment, square, grad, rate, decay):
    moment_after = beta_first * moment + (1.0 - beta_first) * grad
    square_after = beta_second * square + (1.0 - beta_second) * grad * grad
    step_count = STEP
    fixed_moment = moment_after / (1.0 - beta_first**step_count)
    fixed_square = square_after / (1.0 - beta_second**step_count)
    weight_after = weight - rate * (
        fixed_moment / (jnp.sqrt(fixed_square) + adam_eps) + decay * weight
    )
    return (weight_after, moment_after, square_after)


def shards(
    latents,
    pixels,
    visible,
    out_grad,
    panel,
    panel_moment,
    panel_square,
    down,
    down_moment,
    down_square,
    vectors,
    vector_moment,
    vector_square,
):
    images, latent_count, model_width = latents.shape
    pixel_count = pixels.shape[1]
    bf16 = jnp.bfloat16
    full_panel, full_down, full_vector = (
        lax.all_gather(panel.astype(bf16), ("dp", "fsdp"), axis=0, tiled=True),
        lax.all_gather(down.astype(bf16), ("dp", "fsdp"), axis=0, tiled=True),
        lax.all_gather(vectors.astype(bf16), ("dp", "fsdp"), axis=0, tiled=True),
    )
    vector_float = full_vector.astype(jnp.float32)
    gain_pixel = vector_slot(vector_float, 0, model_width)
    shift_pixel = vector_slot(vector_float, 1, model_width)
    gain_cross = vector_slot(vector_float, 2, model_width)
    shift_cross = vector_slot(vector_float, 3, model_width)
    gain_self = vector_slot(vector_float, 4, model_width)
    shift_self = vector_slot(vector_float, 5, model_width)
    gain_feed = vector_slot(vector_float, 6, model_width)
    shift_feed = vector_slot(vector_float, 7, model_width)
    bias_down = vector_slot(vector_float, 8, model_width)
    bias_up = vector_float[9 * model_width :]
    latent_rows = latents.reshape(-1, model_width).astype(jnp.float32)
    pixel_rows = pixels.reshape(-1, model_width).astype(jnp.float32)
    pixel_out, pixel_normed, pixel_inverse = norm_forward(pixel_rows, gain_pixel, shift_pixel)
    pixel_low = pixel_out.astype(bf16)
    cross_out, cross_normed, cross_inverse = norm_forward(latent_rows, gain_cross, shift_cross)
    cross_low = cross_out.astype(bf16)
    cross_queries = matmul_low(cross_low, full_panel[:, :model_width]).astype(bf16)
    pair_rows = matmul_low(pixel_low, full_panel[:, model_width : 3 * model_width]).astype(bf16)
    visible_mask = jnp.arange(pixel_count, dtype=jnp.int32)[None, :] < visible[:, None]
    query_heads = to_heads(cross_queries, images, HEADS)
    key_heads = to_heads(pair_rows[:, :model_width], images, HEADS)
    value_heads = to_heads(pair_rows[:, model_width:], images, HEADS)
    cross_mix, cross_top, cross_total = attend_forward(
        query_heads, key_heads, value_heads, visible_mask
    )
    cross_mixed = cross_mix.reshape(-1, model_width)
    first_sum = latent_rows + matmul_low(
        cross_mixed, full_panel[:, 3 * model_width : 4 * model_width]
    )
    self_columns = full_panel[:, 4 * model_width : 8 * model_width]
    forward_saved = self_forward(first_sum, self_columns, gain_self, shift_self, images)
    second_sum = first_sum + matmul_low(forward_saved[6], self_columns[:, 3 * model_width :])
    feed_out, feed_normed, feed_inverse = norm_forward(second_sum, gain_feed, shift_feed)
    feed_low = feed_out.astype(bf16)
    upper_in = matmul_low(feed_low, full_panel[:, 8 * model_width :]) + bias_up
    hidden_float, gelu_back = jax.vjp(gelu_exact, upper_in)
    hidden = hidden_float.astype(bf16)
    result = second_sum + (matmul_low(hidden, full_down) + bias_down)
    latents_out = result.astype(bf16).reshape(latents.shape)
    grad_three = out_grad.reshape(-1, model_width).astype(jnp.float32)
    grad_branch = grad_three.astype(bf16)
    grad_down = rows_inner(hidden, grad_branch)
    grad_bias_down = jnp.sum(grad_branch.astype(jnp.float32), axis=0)
    grad_upper = gelu_back(times_transposed(grad_branch, full_down))[0].astype(bf16)
    grad_up = rows_inner(feed_low, grad_upper)
    grad_bias_up = jnp.sum(grad_upper.astype(jnp.float32), axis=0)
    grad_feed, grad_gain_feed, grad_shift_feed = norm_backward(
        times_transposed(grad_upper, full_panel[:, 8 * model_width :]),
        feed_normed,
        feed_inverse,
        gain_feed,
    )
    grad_two = grad_three + grad_feed
    again_columns = lax.all_gather(
        panel[:, 4 * model_width : 8 * model_width].astype(bf16), ("dp", "fsdp"), axis=0, tiled=True
    )
    (
        self_normed,
        self_inverse,
        self_low,
        self_queries,
        self_keys,
        self_values,
        self_mixed,
        self_top,
        self_total,
    ) = self_forward(first_sum, again_columns, gain_self, shift_self, images)
    grad_self_branch = grad_two.astype(bf16)
    grad_self_out = rows_inner(self_mixed, grad_self_branch)
    grad_self_mix = times_transposed(grad_self_branch, again_columns[:, 3 * model_width :]).astype(
        bf16
    )
    grad_query_heads, grad_key_heads, grad_value_heads = attend_backward(
        to_heads(grad_self_mix, images, HEADS),
        self_queries,
        self_keys,
        self_values,
        None,
        self_top,
        self_total,
    )
    grad_triple = jnp.concatenate(
        [
            grad_query_heads.reshape(-1, model_width),
            grad_key_heads.reshape(-1, model_width),
            grad_value_heads.reshape(-1, model_width),
        ],
        axis=1,
    ).astype(bf16)
    grad_self_in = rows_inner(self_low, grad_triple)
    grad_first, grad_gain_self, grad_shift_self = norm_backward(
        times_transposed(grad_triple, again_columns[:, : 3 * model_width]),
        self_normed,
        self_inverse,
        gain_self,
    )
    grad_one = grad_two + grad_first
    self_block = jnp.concatenate([grad_self_in, grad_self_out], axis=1)
    grad_cross_branch = grad_one.astype(bf16)
    grad_cross_out = rows_inner(cross_mixed, grad_cross_branch)
    grad_cross_mix = times_transposed(
        grad_cross_branch, full_panel[:, 3 * model_width : 4 * model_width]
    ).astype(bf16)
    cross_query_grad, cross_key_grad, cross_value_grad = attend_backward(
        to_heads(grad_cross_mix, images, HEADS),
        query_heads,
        key_heads,
        value_heads,
        visible_mask,
        cross_top,
        cross_total,
    )
    grad_queries = cross_query_grad.reshape(-1, model_width).astype(bf16)
    grad_pair = jnp.concatenate(
        [cross_key_grad.reshape(-1, model_width), cross_value_grad.reshape(-1, model_width)], axis=1
    ).astype(bf16)
    grad_cross_query = rows_inner(cross_low, grad_queries)
    grad_cross_pair = rows_inner(pixel_low, grad_pair)
    grad_input_norm, grad_gain_cross, grad_shift_cross = norm_backward(
        times_transposed(grad_queries, full_panel[:, :model_width]),
        cross_normed,
        cross_inverse,
        gain_cross,
    )
    pixel_unused, grad_gain_pixel, grad_shift_pixel = norm_backward(
        times_transposed(grad_pair, full_panel[:, model_width : 3 * model_width]),
        pixel_normed,
        pixel_inverse,
        gain_pixel,
    )
    latents_grad = (grad_one + grad_input_norm).reshape(latents.shape)
    vector_grad = jnp.concatenate(
        [
            grad_gain_pixel,
            grad_shift_pixel,
            grad_gain_cross,
            grad_shift_cross,
            grad_gain_self,
            grad_shift_self,
            grad_gain_feed,
            grad_shift_feed,
            grad_bias_down,
            grad_bias_up,
        ]
    )
    cross_block = jnp.concatenate([grad_cross_query, grad_cross_pair, grad_cross_out], axis=1)
    cross_share, self_share, up_share, down_share, vector_share = (
        lax.psum_scatter(cross_block, ("dp", "fsdp"), scatter_dimension=0, tiled=True),
        lax.psum_scatter(self_block, ("dp", "fsdp"), scatter_dimension=0, tiled=True),
        lax.psum_scatter(grad_up, ("dp", "fsdp"), scatter_dimension=0, tiled=True),
        lax.psum_scatter(grad_down, ("dp", "fsdp"), scatter_dimension=0, tiled=True),
        lax.psum_scatter(vector_grad, ("dp", "fsdp"), scatter_dimension=0, tiled=True),
    )
    panel_share = jnp.concatenate([cross_share, self_share, up_share], axis=1)
    local_squares = (
        jnp.sum(panel_share * panel_share)
        + jnp.sum(down_share * down_share)
        + jnp.sum(vector_share * vector_share)
    )
    grad_norm = jnp.sqrt(lax.psum(local_squares, ("dp", "fsdp")))
    device_total = lax.axis_size(("dp", "fsdp"))
    token_total = images * latent_count * device_total
    param_total = (
        model_width * full_panel.shape[1] + full_down.shape[0] * model_width + full_vector.shape[0]
    )
    threshold = clip_coeff * (token_total * param_total) ** 0.5
    factor = threshold / jnp.maximum(grad_norm, threshold)
    panel_after, panel_moment_after, panel_square_after = adam_update(
        panel, panel_moment, panel_square, panel_share * factor, rate_matrix, weight_decay
    )
    down_after, down_moment_after, down_square_after = adam_update(
        down, down_moment, down_square, down_share * factor, rate_matrix, weight_decay
    )
    vectors_after, vector_moment_after, vector_square_after = adam_update(
        vectors, vector_moment, vector_square, vector_share * factor, rate_vector, 0.0
    )
    return (
        latents_out,
        latents_grad,
        grad_norm,
        panel_after,
        panel_moment_after,
        panel_square_after,
        down_after,
        down_moment_after,
        down_square_after,
        vectors_after,
        vector_moment_after,
        vector_square_after,
    )


def solution(mesh):
    placed = (
        P(("dp", "fsdp"), None, None),
        P(("dp", "fsdp"), None, None),
        P(("dp", "fsdp")),
        P(("dp", "fsdp"), None, None),
        P(("dp", "fsdp"), None),
        P(("dp", "fsdp"), None),
        P(("dp", "fsdp"), None),
        P(("dp", "fsdp"), None),
        P(("dp", "fsdp"), None),
        P(("dp", "fsdp"), None),
        P(("dp", "fsdp")),
        P(("dp", "fsdp")),
        P(("dp", "fsdp")),
    )
    return jax.shard_map(
        shards,
        mesh=mesh,
        in_specs=placed,
        out_specs=(
            P(("dp", "fsdp"), None, None),
            P(("dp", "fsdp"), None, None),
            P(),
            P(("dp", "fsdp"), None),
            P(("dp", "fsdp"), None),
            P(("dp", "fsdp"), None),
            P(("dp", "fsdp"), None),
            P(("dp", "fsdp"), None),
            P(("dp", "fsdp"), None),
            P(("dp", "fsdp")),
            P(("dp", "fsdp")),
            P(("dp", "fsdp")),
        ),
        check_vma=False,
    )
```

profile of v0, /device:TPU:0, one launch (start us, length us, event | category | flops | bytes accessed | tf_op | source)
XLA Modules:
  0.0 1889.7 jit_solution(11186028529107525355)
XLA Ops:
  7.3 2.5 convert_element_type.158
  9.8 1.7 slice.138
  11.6 0.7 convert_element_type.174
  13.3 43.5 %all-reduce = bf16[13312]{0:T(1024)(128)(2,1)S(1)} all-reduce(bf16[13312]{0:T(1024)(128)(2,1)S(1)} %dynamic-update-slice), channel_id=1, replica_groups=mesh['dp'=16,'fsdp'=2] {'dp','fsdp'}, use_global_device_ids=true, to_apply=%add | all-reduce | flops 13312 | bytes 53248
  58.2 112.2 %all-gather.4.cloned.1.call-done = bf16[1024,12288]{1,0:T(8,128)(2,1)} async-done(((bf16[32,12288]{1,0:T(8,128)(2,1)}), bf16[1024,12288]{1,0:T(8,128)(2,1)}) %all-gather.4.cloned.1.call-update) | async-done | bytes 25165840 | tf_op jit(solution)/shard_map/all_gather | solution.py:169
  170.5 2.3 fusion.64
  173.0 3.2 fusion.32
  178.0 2.6 fusion.183
  180.9 68.9 %all-gather.8.cloned.1.call-done = bf16[1024,4096]{1,0:T(8,128)(2,1)} async-done(((bf16[32,4096]{1,0:T(8,128)(2,1)}), bf16[1024,4096]{1,0:T(8,128)(2,1)}) %all-gather.8.cloned.1.call-update) | async-done | bytes 8388624 | tf_op jit(solution)/shard_map/all_gather | solution.py:227
  249.8 4.7 fusion.22
  254.5 0.9 fusion.179
  255.4 1.0 copy.102
  256.4 1.0 copy.103
  257.4 4.7 fusion.25
  262.1 0.9 slice_bitcast_fusion.1
  263.2 3.1 fusion.184
  266.4 1.9 convolution_convert_fusion.3
  268.3 2.4 fusion.189
  271.0 15.7 multiply_convert_fusion
  286.7 42.8 %all-gather.6.cloned.1.call-done = bf16[4096,1024]{1,0:T(8,128)(2,1)} async-done(((bf16[128,1024]{1,0:T(8,128)(2,1)}), bf16[4096,1024]{1,0:T(8,128)(2,1)}) %all-gather.6.cloned.1.call-update) | async-done | bytes 8388624 | tf_op jit(solution)/shard_map/all_gather | solution.py:170
  329.5 11.4 convert_reduce_fusion
  341.0 6.3 multiply_reduce_fusion.4
  347.8 0.9 copy-done.4
  348.8 3.2 fusion.70
  351.9 2.0 copy.104
  354.0 2.0 copy.105
  356.0 3.2 fusion.190
  359.2 2.6 multiply_reduce_fusion
  363.9 0.8 slice-done
  364.7 1.6 slice-done.1
  366.3 2.1 multiply_reduce_fusion.5
  368.9 1.0 copy-done.1
  369.8 3.2 fusion.67
  373.0 1.2 copy.106
  374.2 1.6 convolution_convert_fusion.4
  377.7 0.7 fusion.137
  378.4 0.9 fusion.109
  379.3 1.4 fusion.133
  380.8 6.0 pad_maximum_fusion
  387.0 2.2 convolution_convert_fusion.1
  389.2 0.7 fusion.140
  390.6 2.1 fusion.97
  392.6 6.0 pad_maximum_fusion.1
  398.7 9.8 fusion.173
  408.6 1.0 copy-done.10
  409.6 9.7 fusion.117
  419.3 0.9 copy-done.26
  420.3 3.8 fusion.174
  424.1 3.5 fusion.89
  427.6 41.8 %all-reduce.1 = f32[13312]{0:T(1024)S(1)} all-reduce(f32[13312]{0:T(1024)S(1)} %constant_dynamic-update-slice_fusion.6), channel_id=6, replica_groups=mesh['dp'=16,'fsdp'=2] {'dp','fsdp'}, use_global_device_ids=true, to_apply=%region_38.39.clone | all-reduce | flops 13312 | bytes 106496
  470.1 7.2 fusion.80
  477.3 267.0 %reduce-scatter.5.cloned.1.call-done = f32[32,4096]{1,0:T(8,128)} async-done(((f32[1024,4096]{1,0:T(8,128)}), f32[32,4096]{1,0:T(8,128)}) %reduce-scatter.5.cloned.1.call-update) | async-done | bytes 524304 | tf_op jit(solution)/shard_map/reduce_scatter | solution.py:321
  744.3 1.1 constant_dynamic-update-slice_fusion.2
  745.4 359.5 %reduce-scatter.7.cloned.1.call-done = f32[32,4096]{1,0:T(8,128)} async-done(((f32[1024,4096]{1,0:T(8,128)}), f32[32,4096]{1,0:T(8,128)}) %reduce-scatter.7.cloned.1.call-update) | async-done | bytes 524304 | tf_op jit(solution)/shard_map/reduce_scatter | solution.py:322
  1104.9 1.1 constant_dynamic-update-slice_fusion.1
  1106.0 359.6 %reduce-scatter.9.cloned.1.call-done = f32[32,4096]{1,0:T(8,128)} async-done(((f32[1024,4096]{1,0:T(8,128)}), f32[32,4096]{1,0:T(8,128)}) %reduce-scatter.9.cloned.1.call-update) | async-done | bytes 524304 | tf_op jit(solution)/shard_map/reduce_scatter | solution.py:323
  1465.6 1.1 constant_dynamic-update-slice_fusion
  1466.7 1.0 multiply_reduce_fusion.3
  1467.7 358.7 %reduce-scatter.11.cloned.1.call-done = f32[128,1024]{1,0:T(8,128)} async-done(((f32[4096,1024]{1,0:T(8,128)}), f32[128,1024]{1,0:T(8,128)}) %reduce-scatter.11.cloned.1.call-update) | async-done | bytes 524304 | tf_op jit(solution)/shard_map/reduce_scatter | solution.py:324
  1826.4 1.8 multiply_reduce_fusion.14
  1830.1 2.6 fusion.88
  1832.7 40.4 %psum.7 = f32[]{:T(128)} all-reduce(f32[]{:T(128)S(6)} %add.200), channel_id=1, replica_groups=mesh['dp'=16,'fsdp'=2] {'dp','fsdp'}, use_global_device_ids=true, to_apply=%region_40.41 | all-reduce | flops 1 | bytes 8 | tf_op jit(solution)/shard_map/psum | solution.py:333
  1874.6 5.5 multiply_subtract_fusion
  1880.1 1.4 multiply_subtract_fusion.1
  (156 shorter events, 11.6 us)
Async XLA Ops:
  7.2 4.4 copy-start.17
  7.2 5.2 copy-start.40
  7.2 49.6 %copy-start.7 = (bf16[1,128,1024]{2,1,0:T(8,128)(2,1)S(1)}, bf16[1,128,1024]{2,1,0:T(8,128)(2,1)}, u32[]{:S(2)}) copy-start(bf16[1,128,1024]{2,1,0:T(8,128)(2,1)} %param.14) | copy-start | bytes 786436
  7.2 49.9 %copy-start = (bf16[1,256,1024]{2,1,0:T(8,128)(2,1)S(1)}, bf16[1,256,1024]{2,1,0:T(8,128)(2,1)}, u32[]{:S(2)}) copy-start(bf16[1,256,1024]{2,1,0:T(8,128)(2,1)} %param.13) | copy-start | bytes 1572868
  7.2 163.3 %all-gather.4.cloned.1.call-start = ((), (), s32[]{:S(2)}) async-start(), calls=%async_computation.4 | async-start | bytes 25952256 | tf_op jit(solution)/shard_map/all_gather | solution.py:169
  9.7 240.0 %all-gather.8.cloned.1.call-start = ((), (), s32[]{:S(2)}) async-start(), calls=%async_computation.6 | async-start | bytes 8650752 | tf_op jit(solution)/shard_map/all_gather | solution.py:227
  11.5 318.0 %all-gather.6.cloned.1.call-start = ((), (), s32[]{:S(2)}) async-start(), calls=%async_computation.5 | async-start | bytes 8650752 | tf_op jit(solution)/shard_map/all_gather | solution.py:170
  12.3 732.0 %reduce-scatter.5.cloned.1.call-start = ((), (), s32[]{:S(2)}) async-start(), calls=%async_computation.7 | async-start | bytes 17301504 | tf_op jit(solution)/shard_map/reduce_scatter | solution.py:321
  173.0 4.0 copy-start.11
  176.3 4.3 copy-start.38
  176.5 4.1 copy-start.27
  177.0 1.0 copy-start.29
  178.0 71.8 %copy-start.22 = (bf16[8,128,256]{2,1,0:T(8,128)(2,1)}, bf16[8,128,256]{2,1,0:T(8,128)(2,1)S(1)}, u32[]{:S(2)}) copy-start(bf16[8,128,256]{2,1,0:T(8,128)(2,1)S(1)} %convolution_convert_fusion) | copy-start | bytes 1572868
  271.0 58.5 %copy-start.9 = (bf16[1,256,1024]{2,1,0:T(8,128)(2,1)S(1)}, bf16[1,256,1024]{2,1,0:T(8,128)(2,1)}, u32[]{:S(2)}) copy-start(bf16[1,256,1024]{2,1,0:T(8,128)(2,1)} %param.16) | copy-start | bytes 1572868
  341.0 6.3 copy-start.24
  347.8 1.0 copy-start.4
  347.8 8.2 copy-start.20
  359.2 2.6 copy-start.8
  361.8 1.0 copy-start.21
  361.8 1.5 copy-start.33
  361.8 2.9 slice-start
  362.8 1.0 copy-start.13
  362.8 3.4 slice-start.1
  363.3 5.1 copy-start.15
  363.8 4.6 copy-start.31
  366.3 2.2 copy-start.5
  368.9 1.0 copy-start.1
  374.2 1.7 copy-start.30
  374.2 1.7 copy-start.39
  375.9 3.4 copy-start.36
  375.9 1.1 copy-start.12
  375.9 1.4 copy-start.28
  376.0 1.7 copy-start.2
  376.0 1.7 copy-start.23
  377.4 1.9 copy-start.25
  386.8 718.1 %reduce-scatter.7.cloned.1.call-start = ((), (), s32[]{:S(2)}) async-start(), calls=%async_computation.8 | async-start | bytes 17301504 | tf_op jit(solution)/shard_map/reduce_scatter | solution.py:322
  387.0 2.2 copy-start.6
  389.2 1.0 copy-start.14
  389.2 1.2 copy-start.16
  389.2 1.3 copy-start.32
  398.7 1066.9 %reduce-scatter.9.cloned.1.call-start = ((), (), s32[]{:S(2)}) async-start(), calls=%async_computation.9 | async-start | bytes 17301504 | tf_op jit(solution)/shard_map/reduce_scatter | solution.py:323
  408.5 1.0 copy-start.10
  408.6 1417.8 %reduce-scatter.11.cloned.1.call-start = ((), (), s32[]{:S(2)}) async-start(), calls=%async_computation.10 | async-start | bytes 17301504 | tf_op jit(solution)/shard_map/reduce_scatter | solution.py:324
  419.2 0.9 copy-start.26
  419.2 1.0 copy-start.37
  424.0 46.1 %copy-start.42 = (f32[1024]{0:T(1024)S(1)}, f32[1024]{0:T(1024)}, u32[]{:S(2)}) copy-start(f32[1024]{0:T(1024)} %get-tuple-element.47) | copy-start | bytes 12292
  477.3 1352.8 %copy-start.3 = (f32[256,1024]{1,0:T(8,128)S(1)}, f32[256,1024]{1,0:T(8,128)}, u32[]{:S(2)}) copy-start(f32[256,1024]{1,0:T(8,128)} %copy-done.1) | copy-start | bytes 3145732
  745.4 1128.5 %copy-start.41 = (f32[416]{0:T(512)S(1)}, f32[416]{0:T(512)}, u32[]{:S(2)}) copy-start(f32[416]{0:T(512)} %param.23) | copy-start | bytes 4996
  745.4 1128.5 %copy-start.43 = (f32[416]{0:T(512)S(1)}, f32[416]{0:T(512)}, u32[]{:S(2)}) copy-start(f32[416]{0:T(512)} %param.24) | copy-start | bytes 4996
  745.4 1128.5 %copy-start.44 = (f32[416]{0:T(512)S(1)}, f32[416]{0:T(512)}, u32[]{:S(2)}) copy-start(f32[416]{0:T(512)} %param.25) | copy-start | bytes 4996
  1874.6 5.5 copy-start.18
  1874.6 5.5 copy-start.19
  1874.6 5.5 copy-start.34
  1874.6 5.5 copy-start.35
Sparse Core Ops, SparseCore 0:
  11.5 158.9 all-gather.3
  174.1 75.5 all-gather.7
  253.5 76.0 all-gather.5
  386.9 357.3 reduce-scatter.4
  746.5 358.4 reduce-scatter.6
  1107.1 358.4 reduce-scatter.8
  1467.9 358.4 reduce-scatter.10
where the time goes:
time: 1900 us; the launch traced here: 1890 us
  waiting for transfers between devices  1570 us (83%)
  blocking collectives  126 us (7%)
  matrix products  119 us (6%)
  other arithmetic  31.6 us (2%)
  local copies, waits for them, and re-layouts  24.1 us (1%)
  between operations  19.7 us (1%)
    reduce_scatter x1, waiting for transfers between devices, shards(): lax.psum_scatter(grad_up, ('dp', 'fsdp'), scatter_dimension=0, tiled=True)  360 us
    reduce_scatter x1, waiting for transfers between devices, shards(): lax.psum_scatter(self_block, ('dp', 'fsdp'), scatter_dimension=0, tiled=T...  360 us
    reduce_scatter x1, waiting for transfers between devices, shards(): lax.psum_scatter(grad_down, ('dp', 'fsdp'), scatter_dimension=0, tiled=True)  359 us
    reduce_scatter x1, waiting for transfers between devices, shards(): lax.psum_scatter(cross_block, ('dp', 'fsdp'), scatter_dimension=0, tiled=...  267 us
    all_gather x1, waiting for transfers between devices, shards(): lax.all_gather(panel.astype(bf16), ('dp', 'fsdp'), axis=0, tiled=True)  112 us
    unnamed x2, blocking collectives  85.3 us
    all_gather x1, waiting for transfers between devices, shards(): lax.all_gather(panel[:, 4 * model_width:8 * model_width].astype(bf16), ('...  68.9 us
    dot_general x8, matrix products, matmul_low(): return jnp.dot(left, right, preferred_element_type=jnp.float32)  42.8 us
  transfers between devices with their start and end apart: 7, of which 7 were waited for; matrix products, arithmetic and copies ran while one was open for 5% of the time, Pallas kernels for 0%

commit v1 on v0

--- a/solution.py
+++ b/solution.py
@@ -1,6 +1,10 @@
+import functools
+
 import jax
 import jax.numpy as jnp
 from jax import lax
+from jax.experimental import pallas as pl
+from jax.experimental.pallas import tpu as pltpu
 from jax.sharding import PartitionSpec as P
 
 HEADS = 8
@@ -147,7 +151,453 @@
     return (weight_after, moment_after, square_after)
 
 
+MESH = pl.DeviceIdType.MESH
+LONG, SHORT = 4, 2
+CUT = (LONG, SHORT, SHORT, SHORT)
+
+
+class Place:
+    def __init__(self):
+        row, self.y = lax.axis_index("dp"), lax.axis_index("fsdp")
+        self.z, self.x, self.core = row // 4, (row // 2) % 2, row % 2
+        even = self.core == 0
+        x, y = self.x, self.y
+        self.near = (jnp.where(even, 1 - x, x), jnp.where(even, y, 1 - y))
+        self.far = (jnp.where(even, x, 1 - x), jnp.where(even, 1 - y, y))
+        self.first, self.second = jnp.where(even, x, y), jnp.where(even, y, x)
+
+    def device(self, z, x, core, y):
+        return (z * 4 + x * 2 + core, y)
+
+    def along(self, step):
+        return self.device((self.z + step) % LONG, self.x, self.core, self.y)
+
+    def partners(self):
+        return [self.along(step) for step in range(1, LONG)] + [
+            self.device(self.z, self.near[0], self.core, self.near[1]),
+            self.device(self.z, self.far[0], self.core, self.far[1]),
+            self.device(self.z, self.x, 1 - self.core, self.y),
+        ]
+
+    def greet(self):
+        barrier = pltpu.get_barrier_semaphore()
+        for partner in self.partners():
+            pl.semaphore_signal(barrier, inc=1, device_id=partner, device_id_type=MESH)
+        pl.semaphore_wait(barrier, len(self.partners()))
+
+
+def remote(source, target, send, receive, device):
+    return pltpu.make_async_remote_copy(
+        src_ref=source,
+        dst_ref=target,
+        send_sem=send,
+        recv_sem=receive,
+        device_id=device,
+        device_id_type=MESH,
+    )
+
+
+GATHER_KINDS = LONG - 1 + 1 + 2 + 4
+
+
+def gather_kernel(widths, *refs):
+    count = len(widths)
+    shares, wholes = refs[:count], refs[count : 2 * count]
+    send, receive, own = refs[2 * count :]
+    here = Place()
+    z, x, core, y = here.z, here.x, here.core, here.y
+    _, _, _, near, far, twin = here.partners()
+    chunks = []
+    for share, whole, width in zip(shares, wholes, widths):
+        for start in range(0, share.shape[1], width):
+            chunks.append(
+                (share.at[:, pl.ds(start, width)], whole.at[:, :, :, :, :, pl.ds(start, width)])
+            )
+    keep = [
+        pltpu.make_async_copy(share, whole.at[z, x, core, y], own.at[n])
+        for n, (share, whole) in enumerate(zip(shares, wholes))
+    ]
+    for copy in keep:
+        copy.start()
+    here.greet()
+    for copy in keep:
+        copy.wait()
+
+    def copy_of(n, kind, back=False):
+        share, whole = chunks[n]
+        if kind < 3:
+            device, source = here.along(kind + 1), share
+            target = whole.at[z, x, core, y]
+            landing = whole.at[(z - kind - 1) % LONG, x, core, y]
+        else:
+            sets = ((x, y), here.near, here.far, (1 - x, 1 - y))
+            spot = sets[(0, 0, 1, 0, 1, 2, 3)[kind - 3]]
+            source = target = whole.at[:, spot[0], core, spot[1]]
+            device = (near, far, far, twin, twin, twin, twin)[kind - 3]
+            if kind < 6:
+                landed = sets[(1, 2, 3)[kind - 3]]
+                landing = whole.at[:, landed[0], core, landed[1]]
+            else:
+                landed = sets[(0, 2, 1, 3)[kind - 6]]
+                landing = whole.at[:, landed[0], 1 - core, landed[1]]
+        if back:
+            source = target = landing
+        return remote(source, target, send.at[n, kind], receive.at[n, kind], device)
+
+    def start(n, *kinds):
+        for kind in kinds:
+            copy_of(n, kind).start()
+
+    def arrived(n, *kinds):
+        for kind in kinds:
+            copy_of(n, kind, True).wait_recv()
+
+    total = len(chunks)
+    for n in range(min(2, total)):
+        start(n, 0, 1, 2)
+    for tick in range(total + 2):
+        if tick + 2 < total:
+            start(tick + 2, 0, 1, 2)
+        if tick < total:
+            arrived(tick, 0, 1, 2)
+            start(tick, 3, 4, 6)
+        if 0 <= tick - 1 < total:
+            arrived(tick - 1, 3)
+            start(tick - 1, 5, 7)
+        if 0 <= tick - 2 < total:
+            arrived(tick - 2, 4, 5)
+            start(tick - 2, 8, 9)
+    for n in range(total):
+        arrived(n, 6, 7, 8, 9)
+    for n in range(total):
+        for kind in range(GATHER_KINDS):
+            copy_of(n, kind).wait_send()
+
+
+def gather_all(shares, widths):
+    chunks = sum(share.shape[1] // width for share, width in zip(shares, widths))
+    return pl.pallas_call(
+        functools.partial(gather_kernel, tuple(widths)),
+        out_shape=[jax.ShapeDtypeStruct(CUT + share.shape, share.dtype) for share in shares],
+        in_specs=[pl.BlockSpec(memory_space=pl.ANY)] * len(shares),
+        out_specs=[pl.BlockSpec(memory_space=pl.ANY)] * len(shares),
+        scratch_shapes=[
+            pltpu.SemaphoreType.DMA((chunks, GATHER_KINDS)),
+            pltpu.SemaphoreType.DMA((chunks, GATHER_KINDS)),
+            pltpu.SemaphoreType.DMA((len(shares),)),
+        ],
+        compiler_params=pltpu.CompilerParams(collective_id=0, has_side_effects=True),
+    )(*shares)
+
+
+REDUCE_KINDS = 4 + 1 + 1 + 3
+LOADS = 3
+
+
+def reduce_kernel(widths, kinds, *refs):
+    count = len(widths)
+    grads, shares, squares = refs[:count], refs[count : 2 * count], refs[2 * count]
+    scratch = refs[2 * count + 1 :]
+    families = max(kinds) + 1
+    stores = [scratch[5 * k : 5 * k + 5] for k in range(families)]
+    total_ref, meet, send, receive, loaded, meet_send, meet_receive = scratch[5 * families :]
+    here = Place()
+    z, x, core, y = here.z, here.x, here.core, here.y
+    first, second = here.first, here.second
+    _, _, _, near, far, twin = here.partners()
+    here.greet()
+    chunks, used = [], [0] * families
+    for grad, share, width, kind in zip(grads, shares, widths, kinds):
+        for start_at in range(0, grad.shape[5], width):
+            chunks.append((grad, share, start_at, width, stores[kind], used[kind]))
+            used[kind] += 1
+
+    def spot(side, one, two):
+        return jnp.where(side == 0, one, two), jnp.where(side == 0, two, one)
+
+    def load_copies(n):
+        grad, _, start_at, width, store, slot = chunks[n]
+        part = grad.at[:, :, :, :, :, pl.ds(start_at, width)]
+        copies = []
+        for k in range(4):
+            to_x, to_y = spot(core, k // 2, k % 2)
+            copies.append(
+                pltpu.make_async_copy(
+                    part.at[:, to_x, core, to_y],
+                    store[0].at[slot % LOADS, :, k // 2, k % 2],
+                    loaded.at[n, k],
+                )
+            )
+        return copies
+
+    def twin_copies(n):
+        grad, _, start_at, width, store, slot = chunks[n]
+        part = grad.at[:, :, :, :, :, pl.ds(start_at, width)]
+        copies = []
+        for k in range(4):
+            to_x, to_y = spot(1 - core, k // 2, k % 2)
+            copies.append(
+                remote(
+                    part.at[:, to_x, 1 - core, to_y],
+                    store[1].at[slot, :, k // 2, k % 2],
+                    send.at[n, k],
+                    receive.at[n, k],
+                    twin,
+                )
+            )
+        return copies
+
+    def far_copy(n):
+        store, slot = chunks[n][4:]
+        return remote(
+            store[1].at[slot, :, :, 1 - second],
+            store[2].at[slot],
+            send.at[n, 4],
+            receive.at[n, 4],
+            far,
+        )
+
+    def near_copy(n):
+        store, slot = chunks[n][4:]
+        return remote(
+            store[2].at[slot, :, 1 - first],
+            store[3].at[slot],
+            send.at[n, 5],
+            receive.at[n, 5],
+            near,
+        )
+
+    def long_copies(n):
+        store, slot = chunks[n][4:]
+        return [
+            remote(
+                store[3].at[slot, (z + step) % LONG],
+                store[4].at[slot, step - 1],
+                send.at[n, 5 + step],
+                receive.at[n, 5 + step],
+                here.along(step),
+            )
+            for step in range(1, LONG)
+        ]
+
+    def add_up(target, source):
+        target[...] = (target[...].astype(jnp.float32) + source[...].astype(jnp.float32)).astype(
+            target.dtype
+        )
+
+    def begin(n):
+        for copy in load_copies(n) + twin_copies(n):
+            copy.start()
+
+    def stage_twin(n):
+        store, slot = chunks[n][4:]
+        for copy in load_copies(n):
+            copy.wait()
+        for copy in twin_copies(n):
+            copy.wait_recv()
+
+        def one(at, carry):
+            a, b, c = at // 4, (at // 2) % 2, at % 2
+            add_up(store[1].at[slot, a, b, c], store[0].at[slot % LOADS, a, b, c])
+            return carry
+
+        lax.fori_loop(0, 16, one, 0)
+        far_copy(n).start()
+
+    def stage_far(n):
+        store, slot = chunks[n][4:]
+        far_copy(n).wait_recv()
+
+        def one(at, carry):
+            a, b = at // 2, at % 2
+            add_up(store[2].at[slot, a, b], store[1].at[slot, a, b, second])
+            return carry
+
+        lax.fori_loop(0, 8, one, 0)
+        near_copy(n).start()
+
+    def stage_near(n):
+        store, slot = chunks[n][4:]
+        near_copy(n).wait_recv()
+
+        def one(at, carry):
+            add_up(store[3].at[slot, at], store[2].at[slot, at, first])
+            return carry
+
+        lax.fori_loop(0, 4, one, 0)
+        for copy in long_copies(n):
+            copy.start()
+
+    def stage_long(n):
+        _, share, start_at, width, store, slot = chunks[n]
+        for copy in long_copies(n):
+            copy.wait_recv()
+        rows = share.shape[0]
+        step_rows = min(rows, 32)
+
+        def one(at, carry):
+            lines = pl.ds(pl.multiple_of(at * step_rows, step_rows), step_rows)
+            value = store[3][slot, z, lines, :].astype(jnp.float32)
+            for step in range(LONG - 1):
+                value = value + store[4][slot, step, lines, :].astype(jnp.float32)
+            share[lines, pl.ds(start_at, width)] = value
+            square = value * value
+            gained = total_ref[...]
+            for down_at in range(0, step_rows, 8):
+                for across in range(0, width, 128):
+                    gained = gained + square[down_at : down_at + 8, across : across + 128]
+            total_ref[...] = gained
+            return carry
+
+        lax.fori_loop(0, rows // step_rows, one, 0)
+
+    total_ref[...] = jnp.zeros_like(total_ref)
+    total = len(chunks)
+    for n in range(min(2, total)):
+        begin(n)
+    for tick in range(total + 3):
+        if tick + 2 < total:
+            begin(tick + 2)
+        if tick < total:
+            stage_twin(tick)
+        if 0 <= tick - 1 < total:
+            stage_far(tick - 1)
+        if 0 <= tick - 2 < total:
+            stage_near(tick - 2)
+        if 0 <= tick - 3 < total:
+            stage_long(tick - 3)
+    for n in range(total):
+        for copy in twin_copies(n) + [far_copy(n), near_copy(n)] + long_copies(n):
+            copy.wait_send()
+
+    meet[z] = total_ref[...]
+    copies = [
+        remote(
+            total_ref,
+            meet.at[z],
+            meet_send.at[step - 1],
+            meet_receive.at[step - 1],
+            here.along(step),
+        )
+        for step in range(1, LONG)
+    ]
+    for copy in copies:
+        copy.start()
+    for copy in copies:
+        copy.wait()
+    value = meet[0] + meet[1] + meet[2] + meet[3]
+    for k, partner in enumerate((near, far, twin)):
+        meet[4 + 2 * k] = value
+        copy = remote(
+            meet.at[4 + 2 * k],
+            meet.at[5 + 2 * k],
+            meet_send.at[3 + k],
+            meet_receive.at[3 + k],
+            partner,
+        )
+        copy.start()
+        copy.wait()
+        value = value + meet[5 + 2 * k]
+    squares[...] = value
+
+
+def reduce_all(grads, widths, kinds):
+    counts = [0] * (max(kinds) + 1)
+    shapes = [None] * len(counts)
+    for grad, width, kind in zip(grads, widths, kinds):
+        counts[kind] += grad.shape[5] // width
+        shapes[kind] = ((grad.shape[4], width), grad.dtype)
+    scratch = []
+    for number, (shape, dtype) in zip(counts, shapes):
+        scratch += [
+            pltpu.VMEM((LOADS, LONG, SHORT, SHORT) + shape, dtype),
+            pltpu.VMEM((number, LONG, SHORT, SHORT) + shape, dtype),
+            pltpu.VMEM((number, LONG, SHORT) + shape, dtype),
+            pltpu.VMEM((number, LONG) + shape, dtype),
+            pltpu.VMEM((number, LONG - 1) + shape, dtype),
+        ]
+    chunks = sum(counts)
+    return pl.pallas_call(
+        functools.partial(reduce_kernel, tuple(widths), tuple(kinds)),
+        out_shape=[jax.ShapeDtypeStruct(grad.shape[4:], jnp.float32) for grad in grads]
+        + [jax.ShapeDtypeStruct((8, 128), jnp.float32)],
+        in_specs=[pl.BlockSpec(memory_space=pl.ANY)] * len(grads),
+        out_specs=[pl.BlockSpec(memory_space=pltpu.VMEM)] * (len(grads) + 1),
+        scratch_shapes=scratch
+        + [
+            pltpu.VMEM((8, 128), jnp.float32),
+            pltpu.VMEM((10, 8, 128), jnp.float32),
+            pltpu.SemaphoreType.DMA((chunks, REDUCE_KINDS)),
+            pltpu.SemaphoreType.DMA((chunks, REDUCE_KINDS)),
+            pltpu.SemaphoreType.DMA((chunks, 4)),
+            pltpu.SemaphoreType.DMA((6,)),
+            pltpu.SemaphoreType.DMA((6,)),
+        ],
+        compiler_params=pltpu.CompilerParams(
+            collective_id=1, has_side_effects=True, vmem_limit_bytes=60 * 1024 * 1024
+        ),
+    )(*grads)
+
+
+VECTOR_TILE = (8, 128)
+
+
+def packed(rows):
+    spare = VECTOR_TILE[0] * VECTOR_TILE[1] - rows.shape[-1]
+    return jnp.pad(rows, ((0, 0), (0, spare))).reshape((-1,) + VECTOR_TILE)
+
+
+def fast_gather(panel, down, vectors):
+    model_width = panel.shape[1] // 12
+    bf16 = jnp.bfloat16
+    panel_low = panel.astype(bf16)
+    shares = [packed(vectors[None])[0]]
+    shares += [panel_low[:, k * 4 * model_width : (k + 1) * 4 * model_width] for k in range(3)]
+    shares += [down.astype(bf16)]
+    vector_tiles, *wholes = gather_all(shares, [128] + [model_width] * 3 + [down.shape[1] // 4])
+    full_vector = vector_tiles.reshape(-1, VECTOR_TILE[0] * VECTOR_TILE[1])
+    full_vector = full_vector[:, : vectors.shape[0]].reshape(-1)
+    cross, self_columns, up = [whole.reshape(-1, whole.shape[5]) for whole in wholes[:3]]
+    return cross, self_columns, up, wholes[3].reshape(-1, down.shape[1]), full_vector.astype(bf16)
+
+
+def slow_gather(panel, down, vectors):
+    model_width = panel.shape[1] // 12
+    bf16 = jnp.bfloat16
+    parts = [panel[:, k * 4 * model_width : (k + 1) * 4 * model_width].astype(bf16) for k in range(3)]
+    parts += [down.astype(bf16), vectors.astype(bf16)]
+    return [lax.all_gather(part, ("dp", "fsdp"), axis=0, tiled=True) for part in parts]
+
+
+def cut(grad):
+    return grad.reshape(CUT + (-1, grad.shape[1]))
+
+
+def fast_reduce(pieces, down_grad, vector_grad, share_length):
+    bf16 = jnp.bfloat16
+    model_width = down_grad.shape[1]
+    ordered = [pieces[k] for k in (5, 4, 3, 2, 1, 0)]
+    grads = [cut(down_grad.astype(bf16))] + [cut(piece.astype(bf16)) for piece in ordered]
+    grads.append(packed(vector_grad.reshape(-1, share_length)).reshape(CUT + VECTOR_TILE))
+    widths = [model_width // 4] + [model_width] * len(pieces) + [128]
+    kinds = [0] + [1] * len(pieces) + [2]
+    *shares, squares = reduce_all(grads, widths, kinds)
+    panel_share = jnp.concatenate([shares[k] for k in (6, 5, 4, 3, 2, 1)], axis=1)
+    return panel_share, shares[0], shares[7].reshape(-1)[:share_length], jnp.sum(squares)
+
+
+def slow_reduce(pieces, down_grad, vector_grad, share_length):
+    shares = [
+        lax.psum_scatter(grad, ("dp", "fsdp"), scatter_dimension=0, tiled=True)
+        for grad in (jnp.concatenate(pieces, axis=1), down_grad, vector_grad)
+    ]
+    squares = lax.psum(sum(jnp.sum(share * share) for share in shares), ("dp", "fsdp"))
+    return (*shares, squares)
+
+
 def shards(
+    gather,
+    reduce,
     latents,
     pixels,
     visible,
@@ -165,11 +615,7 @@
     images, latent_count, model_width = latents.shape
     pixel_count = pixels.shape[1]
     bf16 = jnp.bfloat16
-    full_panel, full_down, full_vector = (
-        lax.all_gather(panel.astype(bf16), ("dp", "fsdp"), axis=0, tiled=True),
-        lax.all_gather(down.astype(bf16), ("dp", "fsdp"), axis=0, tiled=True),
-        lax.all_gather(vectors.astype(bf16), ("dp", "fsdp"), axis=0, tiled=True),
-    )
+    cross_columns, self_columns, up_columns, full_down, full_vector = gather(panel, down, vectors)
     vector_float = full_vector.astype(jnp.float32)
     gain_pixel = vector_slot(vector_float, 0, model_width)
     shift_pixel = vector_slot(vector_float, 1, model_width)
@@ -187,8 +633,8 @@
     pixel_low = pixel_out.astype(bf16)
     cross_out, cross_normed, cross_inverse = norm_forward(latent_rows, gain_cross, shift_cross)
     cross_low = cross_out.astype(bf16)
-    cross_queries = matmul_low(cross_low, full_panel[:, :model_width]).astype(bf16)
-    pair_rows = matmul_low(pixel_low, full_panel[:, model_width : 3 * model_width]).astype(bf16)
+    cross_queries = matmul_low(cross_low, cross_columns[:, :model_width]).astype(bf16)
+    pair_rows = matmul_low(pixel_low, cross_columns[:, model_width : 3 * model_width]).astype(bf16)
     visible_mask = jnp.arange(pixel_count, dtype=jnp.int32)[None, :] < visible[:, None]
     query_heads = to_heads(cross_queries, images, HEADS)
     key_heads = to_heads(pair_rows[:, :model_width], images, HEADS)
@@ -198,14 +644,13 @@
     )
     cross_mixed = cross_mix.reshape(-1, model_width)
     first_sum = latent_rows + matmul_low(
-        cross_mixed, full_panel[:, 3 * model_width : 4 * model_width]
-    )
-    self_columns = full_panel[:, 4 * model_width : 8 * model_width]
+        cross_mixed, cross_columns[:, 3 * model_width :]
+    )
     forward_saved = self_forward(first_sum, self_columns, gain_self, shift_self, images)
     second_sum = first_sum + matmul_low(forward_saved[6], self_columns[:, 3 * model_width :])
     feed_out, feed_normed, feed_inverse = norm_forward(second_sum, gain_feed, shift_feed)
     feed_low = feed_out.astype(bf16)
-    upper_in = matmul_low(feed_low, full_panel[:, 8 * model_width :]) + bias_up
+    upper_in = matmul_low(feed_low, up_columns) + bias_up
     hidden_float, gelu_back = jax.vjp(gelu_exact, upper_in)
     hidden = hidden_float.astype(bf16)
     result = second_sum + (matmul_low(hidden, full_down) + bias_down)
@@ -218,15 +663,12 @@
     grad_up = rows_inner(feed_low, grad_upper)
     grad_bias_up = jnp.sum(grad_upper.astype(jnp.float32), axis=0)
     grad_feed, grad_gain_feed, grad_shift_feed = norm_backward(
-        times_transposed(grad_upper, full_panel[:, 8 * model_width :]),
+        times_transposed(grad_upper, up_columns),
         feed_normed,
         feed_inverse,
         gain_feed,
     )
     grad_two = grad_three + grad_feed
-    again_columns = lax.all_gather(
-        panel[:, 4 * model_width : 8 * model_width].astype(bf16), ("dp", "fsdp"), axis=0, tiled=True
-    )
     (
         self_normed,
         self_inverse,
@@ -237,10 +679,10 @@
         self_mixed,
         self_top,
         self_total,
-    ) = self_forward(first_sum, again_columns, gain_self, shift_self, images)
+    ) = forward_saved
     grad_self_branch = grad_two.astype(bf16)
     grad_self_out = rows_inner(self_mixed, grad_self_branch)
-    grad_self_mix = times_transposed(grad_self_branch, again_columns[:, 3 * model_width :]).astype(
+    grad_self_mix = times_transposed(grad_self_branch, self_columns[:, 3 * model_width :]).astype(
         bf16
     )
     grad_query_heads, grad_key_heads, grad_value_heads = attend_backward(
@@ -262,17 +704,16 @@
     ).astype(bf16)
     grad_self_in = rows_inner(self_low, grad_triple)
     grad_first, grad_gain_self, grad_shift_self = norm_backward(
-        times_transposed(grad_triple, again_columns[:, : 3 * model_width]),
+        times_transposed(grad_triple, self_columns[:, : 3 * model_width]),
         self_normed,
         self_inverse,
         gain_self,
     )
     grad_one = grad_two + grad_first
-    self_block = jnp.concatenate([grad_self_in, grad_self_out], axis=1)
     grad_cross_branch = grad_one.astype(bf16)
     grad_cross_out = rows_inner(cross_mixed, grad_cross_branch)
     grad_cross_mix = times_transposed(
-        grad_cross_branch, full_panel[:, 3 * model_width : 4 * model_width]
+        grad_cross_branch, cross_columns[:, 3 * model_width :]
     ).astype(bf16)
     cross_query_grad, cross_key_grad, cross_value_grad = attend_backward(
         to_heads(grad_cross_mix, images, HEADS),
@@ -290,13 +731,13 @@
     grad_cross_query = rows_inner(cross_low, grad_queries)
     grad_cross_pair = rows_inner(pixel_low, grad_pair)
     grad_input_norm, grad_gain_cross, grad_shift_cross = norm_backward(
-        times_transposed(grad_queries, full_panel[:, :model_width]),
+        times_transposed(grad_queries, cross_columns[:, :model_width]),
         cross_normed,
         cross_inverse,
         gain_cross,
     )
     pixel_unused, grad_gain_pixel, grad_shift_pixel = norm_backward(
-        times_transposed(grad_pair, full_panel[:, model_width : 3 * model_width]),
+        times_transposed(grad_pair, cross_columns[:, model_width : 3 * model_width]),
         pixel_normed,
         pixel_inverse,
         gain_pixel,
@@ -316,25 +757,22 @@
             grad_bias_up,
         ]
     )
-    cross_block = jnp.concatenate([grad_cross_query, grad_cross_pair, grad_cross_out], axis=1)
-    cross_share, self_share, up_share, down_share, vector_share = (
-        lax.psum_scatter(cross_block, ("dp", "fsdp"), scatter_dimension=0, tiled=True),
-        lax.psum_scatter(self_block, ("dp", "fsdp"), scatter_dimension=0, tiled=True),
-        lax.psum_scatter(grad_up, ("dp", "fsdp"), scatter_dimension=0, tiled=True),
-        lax.psum_scatter(grad_down, ("dp", "fsdp"), scatter_dimension=0, tiled=True),
-        lax.psum_scatter(vector_grad, ("dp", "fsdp"), scatter_dimension=0, tiled=True),
-    )
-    panel_share = jnp.concatenate([cross_share, self_share, up_share], axis=1)
-    local_squares = (
-        jnp.sum(panel_share * panel_share)
-        + jnp.sum(down_share * down_share)
-        + jnp.sum(vector_share * vector_share)
-    )
-    grad_norm = jnp.sqrt(lax.psum(local_squares, ("dp", "fsdp")))
+    pieces = [
+        grad_cross_query,
+        grad_cross_pair,
+        grad_cross_out,
+        grad_self_in,
+        grad_self_out,
+        grad_up,
+    ]
+    panel_share, down_share, vector_share, squares = reduce(
+        pieces, grad_down, vector_grad, vectors.shape[0]
+    )
+    grad_norm = jnp.sqrt(squares)
     device_total = lax.axis_size(("dp", "fsdp"))
     token_total = images * latent_count * device_total
     param_total = (
-        model_width * full_panel.shape[1] + full_down.shape[0] * model_width + full_vector.shape[0]
+        model_width * panel.shape[1] + full_down.shape[0] * model_width + full_vector.shape[0]
     )
     threshold = clip_coeff * (token_total * param_total) ** 0.5
     factor = threshold / jnp.maximum(grad_norm, threshold)
@@ -379,8 +817,12 @@
         P(("dp", "fsdp")),
         P(("dp", "fsdp")),
     )
+    fast = (mesh.shape["dp"], mesh.shape["fsdp"]) == (LONG * SHORT * SHORT, SHORT)
+    step = functools.partial(
+        shards, fast_gather if fast else slow_gather, fast_reduce if fast else slow_reduce
+    )
     return jax.shard_map(
-        shards,
+        step,
         mesh=mesh,
         in_specs=placed,
         out_specs=(

time: 1900 us -> 513 us (0.27)
  waiting for transfers between devices: 1570 us -> 0 us
  Pallas kernels: 0 us -> 360 us
  blocking collectives: 126 us -> 0 us
    reduce_scatter x4 -> x0, waiting for transfers between devices: 1340 us -> none  [the longest x1 360 us: shards(): lax.psum_scatter(grad_up, ('dp', 'fsdp'), scatter_dimension=0, tiled=True)]
    pallas_call x0 -> x2, Pallas kernels: none -> 360 us  [the longest x1 188 us: gather_all(): pl.pallas_call(functools.partial(gather_kernel, tuple(widths)), out_shape...]
    all_gather x3 -> x0, waiting for transfers between devices: 224 us -> none  [the longest x1 112 us: shards(): lax.all_gather(panel.astype(bf16), ('dp', 'fsdp'), axis=0, tiled=True)]
    unnamed x2 -> x0, blocking collectives: 85.3 us -> none
    psum x1 -> x0, blocking collectives: 40.4 us -> none  [shards(): grad_norm = jnp.sqrt(lax.psum(local_squares, ('dp', 'fsdp')))]
    dot_general x8 -> x7, matrix products: 42.8 us -> 35.4 us  [matmul_low(): return jnp.dot(left, right, preferred_element_type=jnp.float32)]
  transfers between devices with their start and end apart: 7 -> 0, of which waited for: 7 -> 0; matrix products, arithmetic and copies ran while one was open for 5% -> 0% of each run, Pallas kernels for 0% -> 0%
where the time goes in v1:
time: 513 us; the launch traced here: 505 us
  Pallas kernels  360 us (70%)
  matrix products  102 us (20%)
  other arithmetic  20.6 us (4%)
  local copies, waits for them, and re-layouts  17.5 us (3%)
    pallas_call x1, Pallas kernels, gather_all(): pl.pallas_call(functools.partial(gather_kernel, tuple(widths)), out_shape...  188 us
    pallas_call x1, Pallas kernels, reduce_all(): pl.pallas_call(functools.partial(reduce_kernel, tuple(widths), tuple(kind...  172 us
    dot_general x7, matrix products, matmul_low(): return jnp.dot(left, right, preferred_element_type=jnp.float32)  35.4 us
    dot_general x7, matrix products, rows_inner(): lax.dot_general(left, right, (((0,), (0,)), ((), ())), preferred_element_...  28.5 us
    dot_general x7, matrix products, times_transposed(): lax.dot_general(left, right, (((1,), (1,)), ((), ())), preferred_element_...  24.9 us

profile of v1, /device:TPU:0, one launch (start us, length us, event | category | flops | bytes accessed | tf_op | source)
XLA Modules:
  0.0 504.6 jit_solution(1010726824252627076)
XLA Ops:
  1.4 1.1 convert_reduce_fusion.3
  2.5 1.2 fusion.90
  3.6 1.2 convert_reduce_fusion.1
  4.8 1.3 fusion.76
  6.2 1.3 pad.8
  7.5 1.8 convert_element_type.165.refs_4_
  9.3 1.5 convert_element_type.164
  10.7 0.9 fusion.142
  11.6 187.6 %shard_map.220 = (f32[4,2,2,2,8,128]{5,4,3,2,1,0:T(8,128)}, bf16[4,2,2,2,32,4096]{5,4,3,2,1,0:T(8,128)(2,1)}, bf16[4,2,2,2,32,4096]{5,4,3,2,1,0:T(8,128)(2,1)}, ...) custom-call(f32[8,128]{1,0:T(8,128)} %bitcast.248, bf16[32,4096]{1,0:T(8,128)(2,1)} %get-tuple-element.70.refs_1_, ...), custom_call_target="tpu_custom_call" | custom-call | tf_op jit(solution)/shard_map/pallas_call | solution.py:279
  199.2 0.9 convert.35
  200.3 2.3 fusion.50
  202.9 3.2 fusion.19
  206.1 0.7 fusion.143
  207.0 0.5 fusion.145
  207.6 1.5 convolution_convert_fusion.7
  209.1 2.6 fusion.146
  212.0 4.7 fusion.12
  216.7 0.9 fusion.141
  218.1 2.2 fusion.147
  220.2 2.1 convolution_convert_fusion.9
  222.4 2.6 fusion.148
  225.4 16.8 %multiply_convert_fusion = (bf16[256,4096]{1,0:T(8,128)(2,1)S(1)}, f32[256,4096]{1,0:T(8,128)}, f32[256,4096]{1,0:T(8,128)}) fusion(f32[4096]{0:T(1024)S(1)} %slice-done.2, bf16[1024,4096]{1,0:T(8,128)(2,1)} %bitcast.251, f32[256,1024]{1,0:T(8,128)S(1)} %get-tuple-element.91, f32[1024]{0:T(1024)S(1)} %get-tuple-element.76, f32[1024]{0:T(1024)S(1)} %get-tuple-element.77, ...), kind=kOutput, calls=%fused_computation.15 | convolution fusion | flops 2218000384 | bytes 19949568 | tf_op jit(solution)/shard_map/dot_general | solution.py:26
  242.2 7.1 %convert_reduce_fusion = (f32[4096]{0:T(1024)S(1)}, bf16[256,4096]{1,0:T(8,128)(2,1)S(1)}) fusion(f32[256,4096]{1,0:T(8,128)} %get-tuple-element.64, f32[256,4096]{1,0:T(8,128)} %get-tuple-element.92, bf16[4096,1024]{1,0:T(8,128)(2,1)S(1)} %bitcast.257, bf16[1,256,1024]{2,1,0:T(8,128)(2,1)S(1)} %copy-done.9), kind=kOutput, calls=%fused_computation.13 | convolution fusion | flops 2164256768 | bytes 19415040 | tf_op jit(solution)/shard_map/dot_general | solution.py:36
  249.3 3.2 fusion.66
  252.5 2.7 multiply_reduce_fusion.2
  255.2 0.5 convert_reduce_fusion.2
  255.7 1.0 copy-done.3
  256.7 3.2 fusion.56
  259.8 2.0 copy.61
  261.9 2.4 convolution_convert_fusion.8
  264.5 0.4 multiply_reduce_fusion
  265.0 0.4 multiply_convert_fusion.1
  265.4 0.9 copy-done.26
  266.2 0.5 fusion.49
  266.7 0.3 fusion.48
  267.1 1.6 slice-done.1
  268.7 2.1 multiply_reduce_fusion.3
  270.9 0.4 multiply_add_fusion.1
  271.3 0.6 copy-done.14
  271.9 2.0 convolution_convert_fusion.6
  273.9 3.2 fusion.53
  277.1 2.0 copy.62
  279.1 1.8 convolution_convert_fusion.10
  281.0 0.5 multiply_reduce_fusion.4
  281.7 0.4 copy-done.17
  282.1 0.3 fusion.67
  282.8 3.9 fusion.136
  286.7 2.8 fusion.75
  289.6 1.4 fusion.74
  291.2 0.7 copy.66
  291.9 3.4 convolution_convert_fusion.5
  295.3 3.2 convolution_convert_fusion.4
  298.6 4.7 convolution_convert_fusion.2
  303.3 3.4 convolution_convert_fusion.3
  306.8 5.7 %convolution_convert_fusion = bf16[1024,4096]{1,0:T(8,128)(2,1)} fusion(bf16[256,4096]{1,0:T(8,128)(2,1)S(1)} %copy-done.11, f32[256,1024]{1,0:T(8,128)S(1)} %get-tuple-element.91, f32[1024]{0:T(1024)S(1)} %get-tuple-element.76, f32[1024]{0:T(1024)S(1)} %get-tuple-element.77, f32[256]{0:T(256)S(1)} %copy-done.56, f32[256]{0:T(256)S(1)} %copy-done.51), kind=kOutput, calls=%fused_computation.2 | convolution fusion | flops 2152988672 | bytes 11544576 | tf_op jit(solution)/shard_map/dot_general | solution.py:30
  312.5 5.9 %convolution_convert_fusion.1 = bf16[4096,1024]{1,0:T(8,128)(2,1)} fusion(bf16[256,4096]{1,0:T(8,128)(2,1)S(1)} %copy-done.8, bf16[1,256,1024]{2,1,0:T(8,128)(2,1)S(1)} %copy-done.9), kind=kOutput, calls=%fused_computation.3 | convolution fusion | flops 2151677952 | bytes 11010048 | tf_op jit(solution)/shard_map/dot_general | solution.py:30
  318.5 172.3 %shard_map.221 = (f32[128,1024]{1,0:T(8,128)}, f32[32,4096]{1,0:T(8,128)}, f32[32,1024]{1,0:T(8,128)}, f32[32,3072]{1,0:T(8,128)}, f32[32,1024]{1,0:T(8,128)}, /...) custom-call(bf16[4,2,2,2,128,1024]{5,4,3,2,1,0:T(8,128)(2,1)} %bitcast.198, ...), custom_call_target="tpu_custom_call" | custom-call | tf_op jit(solution)/shard_map/pallas_call | solution.py:520
  490.8 1.4 reduce_sum.289
  493.0 1.4 multiply_subtract_fusion.2
  494.5 2.5 multiply_subtract_fusion.1
  497.0 0.9 constant_dynamic-update-slice_fusion.6
  497.9 1.0 constant_dynamic-update-slice_fusion.5
  498.9 1.0 constant_dynamic-update-slice_fusion.3
  500.0 3.0 multiply_subtract_fusion
  (189 shorter events, 2.7 us)
Async XLA Ops:
  0.6 199.7 %copy-start = (bf16[1,256,1024]{2,1,0:T(8,128)(2,1)S(1)}, bf16[1,256,1024]{2,1,0:T(8,128)(2,1)}, u32[]{:S(2)}) copy-start(bf16[1,256,1024]{2,1,0:T(8,128)(2,1)} %param.13) | copy-start | bytes 1572868
  2.4 280.3 %copy-start.62 = (f32[128]{0:T(128)}, f32[128]{0:T(128)S(1)}, u32[]{:S(2)}) copy-start(f32[128]{0:T(128)S(1)} %broadcast_multiply_fusion.9) | copy-start | bytes 1540
  3.6 279.1 %copy-start.64 = (f32[128]{0:T(128)}, f32[128]{0:T(128)S(1)}, u32[]{:S(2)}) copy-start(f32[128]{0:T(128)S(1)} %add_rsqrt_fusion.3) | copy-start | bytes 1540
  4.8 284.7 %copy-start.54 = (f32[256]{0:T(256)}, f32[256]{0:T(256)S(1)}, u32[]{:S(2)}) copy-start(f32[256]{0:T(256)S(1)} %broadcast_multiply_fusion.8) | copy-start | bytes 3076
  6.2 283.4 %copy-start.60 = (f32[256]{0:T(256)}, f32[256]{0:T(256)S(1)}, u32[]{:S(2)}) copy-start(f32[256]{0:T(256)S(1)} %add_rsqrt_fusion.2) | copy-start | bytes 3076
  11.6 191.3 %copy-start.6 = (bf16[1,128,1024]{2,1,0:T(8,128)(2,1)S(1)}, bf16[1,128,1024]{2,1,0:T(8,128)(2,1)}, u32[]{:S(2)}) copy-start(bf16[1,128,1024]{2,1,0:T(8,128)(2,1)} %param.14) | copy-start | bytes 786436
  200.3 5.8 %copy-start.47 = (f32[13312]{0:T(1024)}, f32[13312]{0:T(1024)S(1)}, u32[]{:S(2)}) copy-start(f32[13312]{0:T(1024)S(1)} %reshape.413) | copy-start | bytes 159748
  200.3 5.8 %copy-start.57 = (f32[1024]{0:T(1024)}, f32[1024]{0:T(1024)S(1)}, u32[]{:S(2)}) copy-start(f32[1024]{0:T(1024)S(1)} %get-tuple-element.80) | copy-start | bytes 12292
  202.9 4.7 copy-start.16
  207.0 2.0 copy-start.32
  207.6 4.4 copy-start.34
  209.1 7.6 %copy-start.12 = (bf16[8,128,256]{2,1,0:T(8,128)(2,1)}, bf16[8,128,256]{2,1,0:T(8,128)(2,1)S(1)}, u32[]{:S(2)}) copy-start(bf16[8,128,256]{2,1,0:T(8,128)(2,1)S(1)} %convolution_convert_fusion.7) | copy-start | bytes 1572868
  211.7 59.2 %copy-start.52 = (f32[256]{0:T(256)}, f32[256]{0:T(256)S(1)}, u32[]{:S(2)}) copy-start(f32[256]{0:T(256)S(1)} %broadcast_multiply_fusion.7) | copy-start | bytes 3076
  212.0 58.9 %copy-start.58 = (f32[256]{0:T(256)}, f32[256]{0:T(256)S(1)}, u32[]{:S(2)}) copy-start(f32[256]{0:T(256)S(1)} %add_rsqrt_fusion.1) | copy-start | bytes 3076
  217.8 4.5 copy-start.23
  218.1 4.3 copy-start.25
  222.4 2.9 copy-start.13
  222.4 3.0 slice-start.2
  222.4 19.8 %slice-start.5 = ((s8[8388608]{0:T(1024)(128)(4,1)}), s8[4194304]{0:T(1024)(128)(4,1)S(1)}, s32[]{:S(2)}) async-start(s8[8388608]{0:T(1024)(128)(4,1)} %bitcast.255), calls=%async_computation.5 | async-start | bytes 8388608
  222.4 30.1 %slice-start.3 = ((s8[8388608]{0:T(1024)(128)(4,1)}), s8[4194304]{0:T(1024)(128)(4,1)S(1)}, s32[]{:S(2)}) async-start(s8[8388608]{0:T(1024)(128)(4,1)} %bitcast.252), calls=%async_computation.3 | async-start | bytes 8388608
  225.1 30.1 %copy-start.50 = (f32[256]{0:T(256)}, f32[256]{0:T(256)S(1)}, u32[]{:S(2)}) copy-start(f32[256]{0:T(256)S(1)} %broadcast_multiply_fusion.6) | copy-start | bytes 3076
  225.4 29.9 %copy-start.55 = (f32[256]{0:T(256)}, f32[256]{0:T(256)S(1)}, u32[]{:S(2)}) copy-start(f32[256]{0:T(256)S(1)} %add_rsqrt_fusion) | copy-start | bytes 3076
  225.4 16.8 %copy-start.9 = (bf16[1,256,1024]{2,1,0:T(8,128)(2,1)S(1)}, bf16[1,256,1024]{2,1,0:T(8,128)(2,1)}, u32[]{:S(2)}) copy-start(bf16[1,256,1024]{2,1,0:T(8,128)(2,1)} %param.16) | copy-start | bytes 1572868
  225.4 16.8 %slice-start.6 = ((s8[8388608]{0:T(1024)(128)(4,1)}), s8[4194304]{0:T(1024)(128)(4,1)S(1)}, s32[]{:S(2)}) async-start(s8[8388608]{0:T(1024)(128)(4,1)} %bitcast.255), calls=%async_computation.6 | async-start | bytes 8388608
  225.4 27.1 %slice-start.4 = ((s8[8388608]{0:T(1024)(128)(4,1)}), s8[4194304]{0:T(1024)(128)(4,1)S(1)}, s32[]{:S(2)}) async-start(s8[8388608]{0:T(1024)(128)(4,1)} %bitcast.252), calls=%async_computation.4 | async-start | bytes 8388608
  242.2 7.1 %copy-start.7 = (bf16[256,4096]{1,0:T(8,128)(2,1)}, bf16[256,4096]{1,0:T(8,128)(2,1)S(1)}, u32[]{:S(2)}) copy-start(bf16[256,4096]{1,0:T(8,128)(2,1)S(1)} %get-tuple-element.63) | copy-start | bytes 6291460
  249.3 3.2 copy-start.10
  261.9 2.4 copy-start.15
  261.9 2.5 copy-start.39
  261.9 2.6 copy-start.43
  264.3 2.8 copy-start.36
  264.5 2.6 slice-start
  265.0 3.7 slice-start.1
  266.7 4.1 copy-start.18
  267.0 3.8 copy-start.20
  268.7 2.2 copy-start.4
  282.4 4.3 copy-start.30
  282.7 6.8 %copy-start.27 = (bf16[8,128,256]{2,1,0:T(8,128)(2,1)}, bf16[8,128,256]{2,1,0:T(8,128)(2,1)S(1)}, u32[]{:S(2)}) copy-start(bf16[8,128,256]{2,1,0:T(8,128)(2,1)S(1)} %fusion.59) | copy-start | bytes 1572868
  286.7 2.8 copy-start.2
  291.1 7.4 %copy-start.19 = (bf16[8,128,256]{2,1,0:T(8,128)(2,1)S(1)}, bf16[8,128,256]{2,1,0:T(8,128)(2,1)}, u32[]{:S(2)}) copy-start(bf16[8,128,256]{2,1,0:T(8,128)(2,1)} %copy-done.18) | copy-start | bytes 1572868
  291.1 7.4 %copy-start.21 = (bf16[8,128,256]{2,1,0:T(8,128)(2,1)S(1)}, bf16[8,128,256]{2,1,0:T(8,128)(2,1)}, u32[]{:S(2)}) copy-start(bf16[8,128,256]{2,1,0:T(8,128)(2,1)} %copy-done.20) | copy-start | bytes 1572868
  291.1 7.4 %copy-start.37 = (bf16[8,128,256]{2,1,0:T(8,128)(2,1)S(1)}, bf16[8,128,256]{2,1,0:T(8,128)(2,1)}, u32[]{:S(2)}) copy-start(bf16[8,128,256]{2,1,0:T(8,128)(2,1)} %copy-done.36) | copy-start | bytes 1572868
  291.1 7.4 %copy-start.53 = (f32[256]{0:T(256)S(1)}, f32[256]{0:T(256)}, u32[]{:S(2)}) copy-start(f32[256]{0:T(256)} %copy-done.52) | copy-start | bytes 3076
  291.2 7.4 %copy-start.59 = (f32[256]{0:T(256)S(1)}, f32[256]{0:T(256)}, u32[]{:S(2)}) copy-start(f32[256]{0:T(256)} %copy-done.58) | copy-start | bytes 3076
  298.5 4.8 copy-start.31
  298.6 4.8 copy-start.45
  298.6 4.8 copy-start.63
  298.6 4.8 copy-start.65
  303.3 3.5 copy-start.11
  303.3 3.5 copy-start.51
  303.3 3.5 copy-start.56
  306.8 5.7 %copy-start.8 = (bf16[256,4096]{1,0:T(8,128)(2,1)S(1)}, bf16[256,4096]{1,0:T(8,128)(2,1)}, u32[]{:S(2)}) copy-start(bf16[256,4096]{1,0:T(8,128)(2,1)} %copy-done.7) | copy-start | bytes 6291460
  318.4 174.5 %copy-start.61 = (f32[416]{0:T(512)S(1)}, f32[416]{0:T(512)}, u32[]{:S(2)}) copy-start(f32[416]{0:T(512)} %param.23) | copy-start | bytes 4996
  318.4 174.5 %copy-start.66 = (f32[416]{0:T(512)S(1)}, f32[416]{0:T(512)}, u32[]{:S(2)}) copy-start(f32[416]{0:T(512)} %param.24) | copy-start | bytes 4996
  318.4 174.5 %copy-start.67 = (f32[416]{0:T(512)S(1)}, f32[416]{0:T(512)}, u32[]{:S(2)}) copy-start(f32[416]{0:T(512)} %param.25) | copy-start | bytes 4996
  318.4 176.0 %copy-start.22 = (f32[128,1024]{1,0:T(8,128)S(1)}, f32[128,1024]{1,0:T(8,128)}, u32[]{:S(2)}) copy-start(f32[128,1024]{1,0:T(8,128)} %param.20) | copy-start | bytes 1572868
  318.4 176.0 %copy-start.41 = (f32[128,1024]{1,0:T(8,128)S(1)}, f32[128,1024]{1,0:T(8,128)}, u32[]{:S(2)}) copy-start(f32[128,1024]{1,0:T(8,128)} %param.21) | copy-start | bytes 1572868
  318.5 176.0 %copy-start.42 = (f32[128,1024]{1,0:T(8,128)S(1)}, f32[128,1024]{1,0:T(8,128)}, u32[]{:S(2)}) copy-start(f32[128,1024]{1,0:T(8,128)} %param.22) | copy-start | bytes 1572868
  490.8 8.1 %copy-start.49 = (f32[32,1024]{1,0:T(8,128)S(1)}, f32[32,1024]{1,0:T(8,128)}, u32[]{:S(2)}) copy-start(f32[32,1024]{1,0:T(8,128)} %get-tuple-element.34) | copy-start | bytes 393220
  490.8 9.1 %copy-start.48 = (f32[32,1024]{1,0:T(8,128)S(1)}, f32[32,1024]{1,0:T(8,128)}, u32[]{:S(2)}) copy-start(f32[32,1024]{1,0:T(8,128)} %get-tuple-element.36) | copy-start | bytes 393220
  490.8 9.2 %copy-start.5 = (f32[32,12288]{1,0:T(8,128)S(1)}, f32[32,12288]{1,0:T(8,128)}, u32[]{:S(2)}) copy-start(f32[32,12288]{1,0:T(8,128)} %param.17) | copy-start | bytes 4718596
  493.0 6.9 %copy-start.38 = (f32[32,4096]{1,0:T(8,128)S(1)}, f32[32,4096]{1,0:T(8,128)}, u32[]{:S(2)}) copy-start(f32[32,4096]{1,0:T(8,128)} %get-tuple-element.37) | copy-start | bytes 1572868
  493.0 7.0 %copy-start.28 = (f32[32,12288]{1,0:T(8,128)S(1)}, f32[32,12288]{1,0:T(8,128)}, u32[]{:S(2)}) copy-start(f32[32,12288]{1,0:T(8,128)} %param.18) | copy-start | bytes 4718596
  493.0 7.0 %copy-start.29 = (f32[32,12288]{1,0:T(8,128)S(1)}, f32[32,12288]{1,0:T(8,128)}, u32[]{:S(2)}) copy-start(f32[32,12288]{1,0:T(8,128)} %param.19) | copy-start | bytes 4718596
  (11 other events, 17.1 us)

commit v2 on v0

--- a/solution.py
+++ b/solution.py
@@ -1,6 +1,12 @@
+import functools
+import math
+import types
+
 import jax
 import jax.numpy as jnp
 from jax import lax
+from jax.experimental import pallas as pl
+from jax.experimental.pallas import tpu as pltpu
 from jax.sharding import PartitionSpec as P
 
 HEADS = 8
@@ -147,7 +153,1174 @@
     return (weight_after, moment_after, square_after)
 
 
+MESH = pl.DeviceIdType.MESH
+LONG, SHORT = 4, 2
+CUT = (LONG, SHORT, SHORT, SHORT)
+VMEM_LIMIT = 60 * 1024 * 1024
+
+
+class Place:
+    def __init__(self):
+        row, self.y = lax.axis_index("dp"), lax.axis_index("fsdp")
+        self.z, self.x, self.core = row // 4, (row // 2) % 2, row % 2
+        even = self.core == 0
+        x, y = self.x, self.y
+        self.near = (jnp.where(even, 1 - x, x), jnp.where(even, y, 1 - y))
+        self.far = (jnp.where(even, x, 1 - x), jnp.where(even, 1 - y, y))
+        self.first, self.second = jnp.where(even, x, y), jnp.where(even, y, x)
+        self.near_device = self.device(self.z, self.near[0], self.core, self.near[1])
+        self.far_device = self.device(self.z, self.far[0], self.core, self.far[1])
+        self.twin_device = self.device(self.z, x, 1 - self.core, y)
+        self.up_device = self.device(self.z + 1, x, self.core, y)
+        self.down_device = self.device(self.z - 1, x, self.core, y)
+
+    def device(self, z, x, core, y):
+        return (z * 4 + x * 2 + core, y)
+
+    def along(self, step):
+        return self.device((self.z + step) % LONG, self.x, self.core, self.y)
+
+    def greet(self, everyone_along=False):
+        barrier = pltpu.get_barrier_semaphore()
+
+        def signal(partner):
+            pl.semaphore_signal(barrier, inc=1, device_id=partner, device_id_type=MESH)
+
+        for partner in (self.near_device, self.far_device, self.twin_device):
+            signal(partner)
+        if everyone_along:
+            for step in range(1, LONG):
+                signal(self.along(step))
+            pl.semaphore_wait(barrier, 3 + LONG - 1)
+            return
+        pl.when(self.z < LONG - 1)(lambda: signal(self.up_device))
+        pl.when(self.z > 0)(lambda: signal(self.down_device))
+        at_end = jnp.logical_or(self.z == 0, self.z == LONG - 1)
+        pl.semaphore_wait(barrier, 3 + jnp.where(at_end, 1, 2))
+
+
+def remote(source, target, send, receive, device):
+    return pltpu.make_async_remote_copy(
+        src_ref=source,
+        dst_ref=target,
+        send_sem=send,
+        recv_sem=receive,
+        device_id=device,
+        device_id_type=MESH,
+    )
+
+
+GATHER_KINDS = 4 * (LONG - 1) + 4 + 1 + 2
+GATHER_STAGES = 6
+START, RECEIVE, SENT = range(3)
+
+
+class Gather:
+    def __init__(self, here, chunks, send, receive):
+        self.here, self.chunks, self.send, self.receive = here, chunks, send, receive
+        self.count = len(chunks)
+        self.sets = ((here.x, here.y), here.near, here.far, (1 - here.x, 1 - here.y))
+
+    def line_first(self, n):
+        return n % 3 == 0
+
+    def block(self, n, which, z=slice(None)):
+        x, y = self.sets[which]
+        return self.chunks[n].at[z, x, self.here.core, y]
+
+    def copy(self, n, kind, block, device):
+        return remote(block, block, self.send.at[n, kind], self.receive.at[n, kind], device)
+
+    def hop(self, n, step, action):
+        here, z = self.here, self.here.z
+        for piece in (0,) if self.line_first(n) else (0, 1):
+            kind = 6 * piece + 2 * (step - 1)
+
+            def upward(origin, device):
+                return self.copy(n, kind, self.block(n, piece, origin), device)
+
+            def downward(origin, device):
+                return self.copy(n, kind + 1, self.block(n, piece, origin), device)
+
+            if action == RECEIVE:
+
+                @pl.when(z - step >= 0)
+                def _():
+                    upward(z - step, here.down_device).wait_recv()
+
+                @pl.when(z + step <= LONG - 1)
+                def _():
+                    downward(z + step, here.up_device).wait_recv()
+
+            else:
+
+                @pl.when(jnp.logical_and(z - step + 1 >= 0, z < LONG - 1))
+                def _():
+                    copy = upward(z - step + 1, here.up_device)
+                    copy.start() if action == START else copy.wait_send()
+
+                @pl.when(jnp.logical_and(z + step - 1 <= LONG - 1, z > 0))
+                def _():
+                    copy = downward(z + step - 1, here.down_device)
+                    copy.start() if action == START else copy.wait_send()
+
+    def twin(self, n, which):
+        return self.copy(n, 12 + which, self.block(n, which), self.here.twin_device)
+
+    def twin_back(self, n, which):
+        x, y = self.sets[(0, 2, 1, 3)[which]]
+        block = self.chunks[n].at[:, x, 1 - self.here.core, y]
+        return self.copy(n, 12 + which, block, self.here.twin_device)
+
+    def near(self, n, which):
+        z = slice(None) if self.line_first(n) else self.here.z
+        return self.copy(n, 16, self.block(n, which, z), self.here.near_device)
+
+    def far(self, n, which, back=False):
+        return self.copy(
+            n, 17 + which, self.block(n, which + 2 * back), self.here.far_device
+        )
+
+    def stage(self, n, step):
+        if not 0 <= n < self.count:
+            return
+        if step == 5:
+            for which in range(2):
+                self.far(n, which, True).wait_recv()
+                self.twin(n, 2 + which).start()
+        elif self.line_first(n):
+            if step in (1, 2, 3):
+                self.hop(n, step, RECEIVE)
+            if step < 3:
+                self.hop(n, step + 1, START)
+            elif step == 3:
+                self.near(n, 0).start()
+                self.far(n, 0).start()
+                self.twin(n, 0).start()
+            else:
+                self.near(n, 1).wait_recv()
+                self.far(n, 1).start()
+                self.twin(n, 1).start()
+        elif step == 0:
+            self.near(n, 0).start()
+        else:
+            if step == 1:
+                self.near(n, 1).wait_recv()
+            else:
+                self.hop(n, step - 1, RECEIVE)
+            if step < 4:
+                self.hop(n, step, START)
+            else:
+                for which in range(2):
+                    self.far(n, which).start()
+                    self.twin(n, which).start()
+
+    def whole(self, n):
+        for which in range(4):
+            self.twin_back(n, which).wait_recv()
+
+    def finish(self):
+        for n in range(self.count):
+            for step in range(1, LONG):
+                self.hop(n, step, SENT)
+            self.near(n, 0).wait_send()
+            for which in range(2):
+                self.far(n, which).wait_send()
+            for which in range(4):
+                self.twin(n, which).wait_send()
+
+
+REDUCE_KINDS = 1 + 1 + 2 * (LONG - 1)
+REDUCE_STAGES = 6
+RING = 9
+STAGED = 3
+
+
+class Reduce:
+    def __init__(self, here, r, count, put):
+        self.here, self.r, self.count, self.put = here, r, count, put
+
+    def line_last(self, n):
+        return n % 3 == 0
+
+    def at(self, n):
+        slot = n % RING
+        return slot, slot // 3 if self.line_last(n) else slot // 3 * 2 + slot % 3 - 1
+
+    def copy(self, n, kind, source, target, device):
+        r = self.r
+        return remote(source, target, r.reduce_send.at[n, kind], r.reduce_receive.at[n, kind], device)
+
+    def far(self, n):
+        r, here = self.r, self.here
+        source = r.staged.at[n % STAGED, :, :, 1 - here.second]
+        return self.copy(n, 0, source, r.from_far.at[n % RING], here.far_device)
+
+    def near(self, n):
+        r, here = self.r, self.here
+        slot, index = self.at(n)
+        if self.line_last(n):
+            source, target = r.from_far.at[slot, :, 1 - here.first], r.from_near_line.at[index]
+        else:
+            source, target = r.from_far.at[slot, here.z, 1 - here.first], r.from_near.at[index]
+        return self.copy(n, 1, source, target, here.near_device)
+
+    def line(self, n, place):
+        r = self.r
+        slot, index = self.at(n)
+        return r.from_near_line.at[index, place] if self.line_last(n) else r.from_far.at[slot, place]
+
+    def landing(self, n, kind):
+        r = self.r
+        index = self.at(n)[1]
+        return r.from_line_short.at[index, kind] if self.line_last(n) else r.from_line.at[index, kind]
+
+    def hop(self, n, step, action):
+        here, z, away = self.here, self.here.z, LONG - step
+        kind = 2 * (step - 1)
+
+        @pl.when(z - away >= 0)
+        def _():
+            copy = self.copy(
+                n, 2 + kind, self.line(n, z - away), self.landing(n, kind), here.down_device
+            )
+            copy.start() if action == START else copy.wait_send()
+
+        @pl.when(z + away <= LONG - 1)
+        def _():
+            copy = self.copy(
+                n, 3 + kind, self.line(n, z + away), self.landing(n, kind + 1), here.up_device
+            )
+            copy.start() if action == START else copy.wait_send()
+
+    def hop_in(self, n, step):
+        here, z, away = self.here, self.here.z, LONG - step
+        kind = 2 * (step - 1)
+        for side, place, there, device in (
+            (0, z - away + 1, jnp.logical_and(z < LONG - 1, z - away + 1 >= 0), here.up_device),
+            (1, z + away - 1, jnp.logical_and(z > 0, z + away - 1 <= LONG - 1), here.down_device),
+        ):
+
+            @pl.when(there)
+            def _():
+                landed = self.landing(n, kind + side)
+                self.copy(n, 2 + kind + side, landed, landed, device).wait_recv()
+                total = self.line(n, place)
+                if self.line_last(n):
+                    add_up(total, landed)
+                else:
+                    for part in range(SHORT):
+                        add_up(total.at[part], landed.at[part])
+
+    def credit(self, n, kind, condition=None):
+        if n < RING:
+            return
+
+        def take():
+            pl.semaphore_wait(self.r.credit.at[n - RING, kind], 1)
+
+        take() if condition is None else pl.when(condition)(take)
+
+    def give(self, n):
+        if n + RING >= self.count:
+            return
+        here, r = self.here, self.r
+
+        def signal(kind, device):
+            pl.semaphore_signal(r.credit.at[n, kind], inc=1, device_id=device, device_id_type=MESH)
+
+        self.near(n).wait_send()
+        for step in range(1, LONG):
+            self.hop(n, step, SENT)
+        signal(0, here.far_device)
+        signal(1, here.near_device)
+        pl.when(here.z < LONG - 1)(lambda: signal(2, here.up_device))
+        pl.when(here.z > 0)(lambda: signal(3, here.down_device))
+
+    def first_hop(self, n):
+        self.credit(n, 3, self.here.z < LONG - 1)
+        self.credit(n, 2, self.here.z > 0)
+        self.hop(n, 1, START)
+
+    def free(self, n):
+        if n >= STAGED:
+            self.far(n - STAGED).wait_send()
+
+    def stage(self, n, step):
+        if not 0 <= n < self.count:
+            return
+        r, here = self.r, self.here
+        slot, index = self.at(n)
+        if step == 0:
+            self.credit(n, 0)
+            self.far(n).start()
+            return
+        if step == 1:
+            self.far(n).wait_recv()
+
+            def one(at, carry):
+                add_up(
+                    r.from_far.at[slot, at // 2, at % 2],
+                    r.staged.at[n % STAGED, at // 2, at % 2, here.second],
+                )
+                return carry
+
+            lax.fori_loop(0, LONG * SHORT, one, 0)
+            if self.line_last(n):
+                self.credit(n, 1)
+                self.near(n).start()
+            else:
+                self.first_hop(n)
+        elif self.line_last(n):
+            if step == 2:
+                self.near(n).wait_recv()
+
+                def one(at, carry):
+                    add_up(r.from_near_line.at[index, at], r.from_far.at[slot, at, here.first])
+                    return carry
+
+                lax.fori_loop(0, LONG, one, 0)
+                self.first_hop(n)
+            else:
+                self.hop_in(n, step - 2)
+                if step < 5:
+                    self.hop(n, step - 1, START)
+                else:
+                    self.put(n, r.from_near_line[index, here.z].astype(jnp.float32))
+                    self.give(n)
+        elif step < 5:
+            self.hop_in(n, step - 1)
+            if step < 4:
+                self.hop(n, step, START)
+            else:
+                self.credit(n, 1)
+                self.near(n).start()
+        else:
+            self.near(n).wait_recv()
+            own = r.from_far[slot, here.z, here.first].astype(jnp.float32)
+            self.put(n, own + r.from_near[index].astype(jnp.float32))
+            self.give(n)
+
+    def tick(self, n):
+        for step in range(REDUCE_STAGES):
+            self.stage(n - step, step)
+
+    def finish(self):
+        for n in range(max(0, self.count - STAGED), self.count):
+            self.far(n).wait_send()
+        for n in range(max(0, self.count - RING), self.count):
+            self.near(n).wait_send()
+            for step in range(1, LONG):
+                self.hop(n, step, SENT)
+
+
+def add_up(target, source):
+    total = target[...].astype(jnp.float32) + source[...].astype(jnp.float32)
+    target[...] = total.astype(target.dtype)
+
+
+class Meeting:
+    def __init__(self, here, value, line, pairs, send, receive):
+        self.here, self.value, self.line, self.pairs = here, value, line, pairs
+        self.send, self.receive = send, receive
+
+    def along(self, step, back=False):
+        here = self.here
+        place = (here.z - step) % LONG if back else here.z
+        return remote(
+            self.line.at[place] if back else self.value,
+            self.line.at[place],
+            self.send.at[step - 1],
+            self.receive.at[step - 1],
+            here.along(step),
+        )
+
+    def pair(self, k):
+        here = self.here
+        device = (here.near_device, here.far_device, here.twin_device)[k]
+        return remote(
+            self.pairs.at[2 * k],
+            self.pairs.at[2 * k + 1],
+            self.send.at[LONG - 1 + k],
+            self.receive.at[LONG - 1 + k],
+            device,
+        )
+
+    def step(self, k):
+        if k == 0:
+            self.line[self.here.z] = self.value[...]
+            for away in range(1, LONG):
+                self.along(away).start()
+            return None
+        if k == 1:
+            for away in range(1, LONG):
+                self.along(away).wait_send()
+                self.along(away, True).wait_recv()
+            total = self.line[0]
+            for place in range(1, LONG):
+                total = total + self.line[place]
+        else:
+            self.pair(k - 2).wait()
+            total = self.pairs[2 * k - 4] + self.pairs[2 * k - 3]
+        if k < 4:
+            self.pairs[2 * k - 2] = total
+            self.pair(k - 1).start()
+        return total
+
+
+TILE = 256
+LANES = 128
+BAND = 32
+CROSS_Q, CROSS_K, CROSS_V, CROSS_O, SELF_Q, SELF_K, SELF_V, SELF_O, UP = range(9)
+
+
+def tile(start, size):
+    return pl.ds(pl.multiple_of(start, size), size)
+
+
+def bands(rows, body, carry=0):
+    return lax.fori_loop(0, rows // BAND, lambda k, c: body(tile(k * BAND, BAND), c), carry)
+
+
+def normalised(values):
+    centre = values - jnp.mean(values, axis=-1, keepdims=True)
+    inverse = lax.rsqrt(jnp.mean(centre * centre, axis=-1, keepdims=True) + norm_eps)
+    return centre * inverse, inverse
+
+
+def block_kernel(names, sizes, *refs):
+    r = types.SimpleNamespace(**dict(zip(names, refs, strict=True)))
+    width, lat, pix, hidden_parts = sizes
+    f32, bf16 = jnp.float32, jnp.bfloat16
+    here = Place()
+    core = here.core
+    scale = (width // HEADS) ** (-0.5)
+    panel_blocks = UP + hidden_parts
+    gather_order = [CROSS_K, CROSS_V, CROSS_Q, CROSS_O, SELF_Q, SELF_K, SELF_V, SELF_O]
+    gather_order += list(range(UP, panel_blocks))
+    share_rows = r.panel.shape[0]
+
+    meet_in = Meeting(here, r.vectors, r.meet_line, r.meet_pairs, r.meet_send, r.meet_receive)
+    meet_out = Meeting(here, r.vector_grad, r.sum_line, r.sum_pairs, r.sum_send, r.sum_receive)
+    meet_last = Meeting(here, r.squares, r.last_line, r.last_pairs, r.last_send, r.last_receive)
+
+    chunks, keep = [], []
+    for block in gather_order:
+        columns = pl.ds(block * width, width)
+        r.low_panel[:, columns] = r.panel[:, columns].astype(bf16)
+        whole = r.whole_panel.at[:, :, :, :, :, columns]
+        chunks.append(whole)
+        own = whole.at[here.z, here.x, core, here.y]
+        keep.append(pltpu.make_async_copy(r.low_panel.at[:, columns], own, r.own.at[len(keep)]))
+        keep[-1].start()
+    for part in range(hidden_parts):
+        rows = pl.ds(part * share_rows, share_rows)
+        r.low_down[rows, :] = r.down[rows, :].astype(bf16)
+        whole = r.whole_down.at[:, :, :, :, rows]
+        chunks.append(whole)
+        own = whole.at[here.z, here.x, core, here.y]
+        keep.append(pltpu.make_async_copy(r.low_down.at[rows], own, r.own.at[len(keep)]))
+        keep[-1].start()
+    gather = Gather(here, chunks, r.gather_send, r.gather_receive)
+    here.greet(True)
+
+    def gather_tick(tick):
+        if tick < len(keep):
+            keep[tick].wait()
+        for step in range(GATHER_STAGES):
+            gather.stage(tick - step, step)
+
+    twins = {}
+
+    def to_twin(source, target):
+        number = len(twins)
+        copy = remote(
+            source, target, r.twin_send.at[number], r.twin_receive.at[number], here.twin_device
+        )
+        copy.start()
+        twins[number] = copy
+        return number
+
+    def from_twin(number):
+        twins[number].wait_recv()
+
+    flat_panel = r.whole_panel.reshape(-1, panel_blocks * width)
+    flat_down = r.whole_down.reshape(-1, width)
+    loads = []
+
+    def fetch(part):
+        if isinstance(part, tuple):
+            source = flat_down.at[pl.ds(part[1] * width, width)]
+        else:
+            source = flat_panel.at[:, pl.ds(part * width, width)]
+        slot = len(loads) % 2
+        copy = pltpu.make_async_copy(source, r.weights.at[slot], r.load.at[slot])
+        copy.start()
+        loads.append(copy)
+        return len(loads) - 1
+
+    def fetched(number):
+        loads[number].wait()
+        return number % 2
+
+    def put(n, value):
+        if n < hidden_parts:
+            r.down_share[n * share_rows : (n + 1) * share_rows, :] = value
+        else:
+            block = reduce_order[n]
+            r.panel_share[:, block * width : (block + 1) * width] = value
+        square = value * value
+        gained = r.squares[...]
+        for across in range(0, width, LANES):
+            for at in range(0, share_rows, 8):
+                gained = gained + square[at : at + 8, across : across + LANES]
+        r.squares[...] = gained
+
+    reduce_order = [None] * hidden_parts + list(range(UP, panel_blocks))
+    reduce_order += [SELF_O, SELF_Q, SELF_K, SELF_V, CROSS_O, CROSS_Q, CROSS_K, CROSS_V]
+    reduce = Reduce(here, r, len(reduce_order), put)
+
+    def vector(k):
+        return r.rows[k : k + 1, :]
+
+    def times(left, slot, emit):
+        def one(k, carry):
+            columns = tile(k * TILE, TILE)
+            emit(columns, jnp.dot(left[...], r.weights[slot, :, columns], preferred_element_type=f32))
+            return carry
+
+        lax.fori_loop(0, width // TILE, one, 0)
+
+    def times_back(left, slot, emit):
+        def one(k, carry):
+            columns = tile(k * TILE, TILE)
+            emit(columns, times_transposed(left[...], r.weights[slot, columns, :]))
+            return carry
+
+        lax.fori_loop(0, width // TILE, one, 0)
+
+    def norm_rows(read, count, gain, shift, target):
+        def one(rows, carry):
+            normed, _ = normalised(read(rows))
+            target[rows, :] = (normed * vector(gain) + vector(shift)).astype(bf16)
+            return carry
+
+        bands(count, one)
+
+    def keep_vector(k, value):
+        for at in range(width // LANES):
+            row = k * (width // LANES) + at
+            r.vector_grad[row : row + 1, :] = value[:, at * LANES : (at + 1) * LANES]
+
+    def folded(value):
+        total = value[0:8]
+        for at in range(8, BAND, 8):
+            total = total + value[at : at + 8]
+        return total
+
+    def norm_back(read, grad, count, gain, shift, emit):
+        def one(rows, carry):
+            gain_sum, shift_sum = carry
+            normed, inverse = normalised(read(rows))
+            out = grad[rows, :]
+            if emit is not None:
+                inner = out * vector(gain)
+                emit(
+                    rows,
+                    inverse
+                    * (
+                        inner
+                        - jnp.mean(inner, axis=-1, keepdims=True)
+                        - normed * jnp.mean(inner * normed, axis=-1, keepdims=True)
+                    ),
+                )
+            return gain_sum + folded(out * normed), shift_sum + folded(out)
+
+        empty = jnp.zeros((8, width), f32)
+        gain_sum, shift_sum = bands(count, one, (empty, empty))
+        keep_vector(gain, jnp.sum(gain_sum, axis=0, keepdims=True))
+        keep_vector(shift, jnp.sum(shift_sum, axis=0, keepdims=True))
+
+    head = width // HEADS
+
+    def probabilities(queries, keys, masked):
+        scores = times_transposed(queries, keys) * scale
+        if masked:
+            scores = jnp.where(r.mask[0:1, :] > 0.5, scores, masked_fill)
+        powers = jnp.exp(scores - jnp.max(scores, axis=-1, keepdims=True))
+        return powers / jnp.sum(powers, axis=-1, keepdims=True)
+
+    def attend(queries, keys, key_start, values, value_start, masked, target):
+        def one(k, carry):
+            columns = tile(k * head, head)
+            probability = probabilities(
+                queries[:, columns], keys[:, tile(key_start + k * head, head)], masked
+            )
+            value_rows = values[:, tile(value_start + k * head, head)]
+            target[:, columns] = matmul_low(probability.astype(bf16), value_rows).astype(bf16)
+            return carry
+
+        lax.fori_loop(0, HEADS, one, 0)
+
+    def attend_back(grad, queries, keys, key_start, values, value_start, masked, targets):
+        query_grad, key_grad, key_at, value_grad, value_at = targets
+
+        def one(k, carry):
+            columns = tile(k * head, head)
+            key_columns = tile(key_start + k * head, head)
+            value_columns = tile(value_start + k * head, head)
+            query_rows, key_rows = queries[:, columns], keys[:, key_columns]
+            probability = probabilities(query_rows, key_rows, masked)
+            grad_mix = grad[:, columns]
+            grad_prob = times_transposed(grad_mix, values[:, value_columns])
+            inner = jnp.sum(grad_prob * probability, axis=-1, keepdims=True)
+            grad_scores = (probability * (grad_prob - inner)).astype(bf16)
+            query_grad[:, columns] = (matmul_low(grad_scores, key_rows) * scale).astype(bf16)
+            key_grad[:, tile(key_at + k * head, head)] = (
+                rows_inner(grad_scores, query_rows) * scale
+            ).astype(bf16)
+            value_grad[:, tile(value_at + k * head, head)] = rows_inner(
+                probability.astype(bf16), grad_mix
+            ).astype(bf16)
+            return carry
+
+        lax.fori_loop(0, HEADS, one, 0)
+
+    row_id = lax.broadcasted_iota(jnp.int32, (LANES, LANES), 0)
+    unit = (row_id == lax.broadcasted_iota(jnp.int32, (LANES, LANES), 1)).astype(bf16)
+
+    def turn(source, target, landing):
+        def one(k, carry):
+            turned = times_transposed(unit, source[:, tile(k * LANES, LANES)]).astype(bf16)
+            for side in range(2):
+                target[side, k] = turned[side * LANES // 2 : (side + 1) * LANES // 2]
+            return carry
+
+        lax.fori_loop(0, width // LANES, one, 0)
+        return to_twin(target.at[1 - core], landing)
+
+    def weight_grad(n, own, other, grad, grad_other, start):
+        reduce.free(n)
+        slot = n % STAGED
+
+        def one(k, carry):
+            columns = tile(start + k * TILE, TILE)
+            total = matmul_low(own(), grad[:, columns]) + matmul_low(other(), grad_other[:, columns])
+            total = total.astype(bf16).reshape(LONG, SHORT, SHORT, share_rows, TILE)
+            into = tile(k * TILE, TILE)
+            for to_x in range(SHORT):
+                for to_y in range(SHORT):
+                    first = jnp.where(core == 0, to_x, to_y)
+                    second = jnp.where(core == 0, to_y, to_x)
+                    r.staged[slot, :, first, second, :, into] = total[:, to_x, to_y]
+            return carry
+
+        lax.fori_loop(0, width // TILE, one, 0)
+
+    def turned_pair(target, landing):
+        rows = target.shape[3]
+        return (
+            lambda: target[core].reshape(-1, rows),
+            lambda: landing[...].reshape(-1, rows),
+        )
+
+    dz_sent = None
+    marks = types.SimpleNamespace()
+
+    def after_vectors(total):
+        per = width // LANES
+        for row in range(r.rows.shape[0]):
+            for at in range(per):
+                line = total[row * per + at : row * per + at + 1, :]
+                r.rows[row : row + 1, at * LANES : (at + 1) * LANES] = line.astype(bf16).astype(f32)
+        norm_rows(lambda rows: r.pixels[rows, :].astype(f32), pix, 0, 1, r.pixel_low)
+        norm_rows(lambda rows: r.latents[rows, :].astype(f32), lat, 2, 3, r.left)
+        marks.pixel = turn(r.pixel_low, r.turned_pixel, r.landed_pixel)
+        marks.cross = turn(r.left, r.turned_cross, r.landed_cross)
+
+    def to_columns(target, start=0):
+        def emit(columns, value):
+            where = pl.ds(pl.multiple_of(columns.start + start, TILE), TILE)
+            target[:, where] = value.astype(bf16)
+
+        return emit
+
+    def add_columns(target, base):
+        def emit(columns, value):
+            target[:, columns] = base[:, columns].astype(f32) + value
+
+        return emit
+
+    def forward(block, slot):
+        if block == CROSS_K:
+            times(r.pixel_low, slot, to_columns(r.pair))
+        elif block == CROSS_V:
+            times(r.pixel_low, slot, to_columns(r.pair, width))
+        elif block == CROSS_Q:
+            times(r.left, slot, to_columns(r.cross_query))
+            attend(r.cross_query, r.pair, 0, r.pair, width, True, r.mixed)
+            marks.cross_mix = turn(r.mixed, r.turned_cross_mix, r.landed_cross_mix)
+        elif block == CROSS_O:
+            times(r.mixed, slot, add_columns(r.first, r.latents))
+            norm_rows(lambda rows: r.first[rows, :], lat, 4, 5, r.left)
+            marks.self = turn(r.left, r.turned_self, r.landed_self)
+        elif block in (SELF_Q, SELF_K, SELF_V):
+            times(r.left, slot, to_columns(r.triple, (block - SELF_Q) * width))
+            if block == SELF_V:
+                attend(r.triple, r.triple, width, r.triple, 2 * width, False, r.mixed)
+                marks.self_mix = turn(r.mixed, r.turned_self_mix, r.landed_self_mix)
+        elif block == SELF_O:
+            times(r.mixed, slot, add_columns(r.second, r.first))
+            norm_rows(lambda rows: r.second[rows, :], lat, 6, 7, r.left)
+            marks.feed = turn(r.left, r.turned_feed, r.landed_feed)
+        else:
+            part = block - UP
+
+            def emit(columns, value):
+                upper = value + r.rows[9 + part : 10 + part, columns]
+                below = 0.5 + 0.5 * lax.erf(upper * (0.5**0.5))
+                where = pl.ds(pl.multiple_of(columns.start + part * width, TILE), TILE)
+                r.hidden[:, where] = (upper * below).astype(bf16)
+                density = jnp.exp(-0.5 * upper * upper) * ((2.0 * math.pi) ** -0.5)
+                r.slope[:, where] = below + upper * density
+
+            times(r.left, slot, emit)
+
+            def one(k, carry):
+                block_at = part * (width // LANES) + k
+                turned = times_transposed(unit, r.hidden[:, tile(block_at * LANES, LANES)])
+                turned = turned.astype(bf16).reshape(hidden_parts, share_rows, lat)
+                side = (k // 2) % 2
+                r.turned_hidden[side, block_at // 4 * 2 + k % 2] = turned
+                return carry
+
+            lax.fori_loop(0, width // LANES, one, 0)
+
+    ticks = len(chunks) + GATHER_STAGES - 1
+    lead = GATHER_STAGES + 1
+    forward_blocks = len(gather_order)
+    for tick in range(forward_blocks + lead):
+        gather_tick(tick)
+        if tick < 5:
+            total = meet_in.step(tick)
+            if tick == 4:
+                after_vectors(total)
+        elif tick == 5:
+            marks.dz = to_twin(r.out_grad, r.landed_dz)
+        if 0 <= tick - lead + 1 < forward_blocks:
+            gather.whole(tick - lead + 1)
+            fetch(gather_order[tick - lead + 1])
+        if tick - lead >= 0:
+            forward(gather_order[tick - lead], fetched(tick - lead))
+    marks.hidden = to_twin(r.turned_hidden.at[1 - core], r.landed_hidden)
+
+    r.squares[...] = jnp.zeros_like(r.squares)
+    for tick in range(forward_blocks + lead, ticks):
+        gather_tick(tick)
+    from_twin(marks.dz)
+    from_twin(marks.hidden)
+
+    def hidden_grad(part):
+        weight_grad(
+            part,
+            lambda: r.turned_hidden[core, :, part].reshape(-1, lat),
+            lambda: r.landed_hidden[:, part].reshape(-1, lat),
+            r.out_grad,
+            r.landed_dz,
+            0,
+        )
+        reduce.tick(part)
+
+    hidden_grad(0)
+    for n in range(forward_blocks, len(chunks)):
+        gather.whole(n)
+    number = fetch(("down", 0))
+    hidden_grad(1)
+
+    def start_out(rows, carry):
+        r.total[rows, :] = r.second[rows, :] + vector(8)
+        return carry + folded(r.out_grad[rows, :].astype(f32))
+
+    shift_sum = bands(lat, start_out, jnp.zeros((8, width), f32))
+    keep_vector(8, jnp.sum(shift_sum, axis=0, keepdims=True))
+    du_marks = []
+
+    def out_and_du(part, slot):
+        hidden_part = r.hidden.at[:, pl.ds(part * width, width)]
+
+        def emit(columns, value):
+            r.total[:, columns] += value
+
+        times(hidden_part, slot, emit)
+
+        def emit_du(columns, value):
+            where = pl.ds(pl.multiple_of(columns.start + part * width, TILE), TILE)
+            low = (value * r.slope[:, where]).astype(bf16)
+            r.hidden[:, where] = low
+            column_sum = jnp.sum(low.astype(f32), axis=0, keepdims=True)
+            at = 9 * (width // LANES) + part * (width // LANES) + lax.div(columns.start, LANES)
+            for k in range(TILE // LANES):
+                r.vector_grad[pl.ds(at + k, 1), :] = column_sum[:, k * LANES : (k + 1) * LANES]
+
+        times_back(r.out_grad, slot, emit_du)
+        du_marks.append(to_twin(hidden_part, r.landed_du.at[:, pl.ds(part * width, width)]))
+
+    for part in range(hidden_parts):
+        slot = fetched(number)
+        number = fetch(("down", part + 1) if part + 1 < hidden_parts else UP)
+        out_and_du(part, slot)
+        if part + 2 < hidden_parts:
+            hidden_grad(part + 2)
+
+    def finish_out(rows, carry):
+        r.latents_out[rows, :] = r.total[rows, :].astype(bf16)
+        r.total[rows, :] = jnp.zeros((BAND, width), f32)
+        return carry
+
+    bands(lat, finish_out)
+
+    def add_total(columns, value):
+        r.total[:, columns] += value
+
+    from_twin(marks.feed)
+    own, other = turned_pair(r.turned_feed, r.landed_feed)
+    for part in range(hidden_parts):
+        slot = fetched(number)
+        number = fetch(UP + part + 1 if part + 1 < hidden_parts else SELF_O)
+        times_back(r.hidden.at[:, pl.ds(part * width, width)], slot, add_total)
+        from_twin(du_marks[part])
+        n = hidden_parts + part
+        weight_grad(n, own, other, r.hidden, r.landed_du, part * width)
+        if part + 1 == hidden_parts:
+
+            def into_second(rows, value):
+                value = value + r.out_grad[rows, :].astype(f32)
+                r.second[rows, :] = value
+                r.grad_low[rows, :] = value.astype(bf16)
+
+            norm_back(lambda rows: r.second[rows, :], r.total, lat, 6, 7, into_second)
+            marks.ds = to_twin(r.grad_low, r.landed_ds)
+        reduce.tick(n)
+
+    def branch_out(n, slot, grad_low, landed, mark, turned, landed_turned, turned_mark):
+        times_back(grad_low, slot, to_columns(r.mixed))
+        from_twin(mark)
+        from_twin(turned_mark)
+        weight_grad(n, *turned_pair(turned, landed_turned), grad_low, landed, 0)
+
+    n = 2 * hidden_parts
+    slot = fetched(number)
+    number = fetch(SELF_Q)
+    branch_out(
+        n, slot, r.grad_low, r.landed_ds, marks.ds, r.turned_self_mix, r.landed_self_mix, marks.self_mix
+    )
+    reduce.stage(n, 0)
+    attend_back(
+        r.mixed,
+        r.triple,
+        r.triple,
+        width,
+        r.triple,
+        2 * width,
+        False,
+        (r.triple_grad, r.triple_grad, width, r.triple_grad, 2 * width),
+    )
+    triple_marks = []
+    for part in range(3):
+        columns = pl.ds(part * width, width)
+        triple_marks.append(to_twin(r.triple_grad.at[:, columns], r.landed_triple.at[:, columns]))
+    for step in range(1, REDUCE_STAGES):
+        reduce.stage(n - step, step)
+
+    def clear(rows, carry):
+        r.total[rows, :] = jnp.zeros((BAND, width), f32)
+        return carry
+
+    bands(lat, clear)
+    from_twin(marks.self)
+    own, other = turned_pair(r.turned_self, r.landed_self)
+    for part in range(3):
+        slot = fetched(number)
+        number = fetch((SELF_K, SELF_V, CROSS_O)[part])
+        times_back(r.triple_grad.at[:, pl.ds(part * width, width)], slot, add_total)
+        from_twin(triple_marks[part])
+        n += 1
+        weight_grad(n, own, other, r.triple_grad, r.landed_triple, part * width)
+        if part == 2:
+
+            def into_first(rows, value):
+                value = value + r.second[rows, :]
+                r.second[rows, :] = value
+                r.cross_low[rows, :] = value.astype(bf16)
+
+            norm_back(lambda rows: r.first[rows, :], r.total, lat, 4, 5, into_first)
+            marks.dc = to_twin(r.cross_low, r.landed_dc)
+        reduce.tick(n)
+
+    n += 1
+    slot = fetched(number)
+    number = fetch(CROSS_Q)
+    branch_out(
+        n, slot, r.cross_low, r.landed_dc, marks.dc, r.turned_cross_mix, r.landed_cross_mix, marks.cross_mix
+    )
+    reduce.stage(n, 0)
+    attend_back(
+        r.mixed,
+        r.cross_query,
+        r.pair,
+        0,
+        r.pair,
+        width,
+        True,
+        (r.query_grad, r.pair_grad, 0, r.pair_grad, width),
+    )
+    query_mark = to_twin(r.query_grad, r.landed_query)
+    pair_marks = []
+    for part in range(2):
+        columns = pl.ds(part * width, width)
+        pair_marks.append(to_twin(r.pair_grad.at[:, columns], r.landed_pair.at[:, columns]))
+    for step in range(1, REDUCE_STAGES):
+        reduce.stage(n - step, step)
+
+    slot = fetched(number)
+    number = fetch(CROSS_K)
+
+    def set_total(columns, value):
+        r.total[:, columns] = value
+
+    times_back(r.query_grad, slot, set_total)
+    from_twin(query_mark)
+    from_twin(marks.cross)
+    n += 1
+    weight_grad(n, *turned_pair(r.turned_cross, r.landed_cross), r.query_grad, r.landed_query, 0)
+    reduce.stage(n, 0)
+
+    def into_latents(rows, value):
+        r.latents_grad[rows, :] = value + r.second[rows, :]
+
+    norm_back(lambda rows: r.latents[rows, :].astype(f32), r.total, lat, 2, 3, into_latents)
+    for step in range(1, REDUCE_STAGES):
+        reduce.stage(n - step, step)
+    from_twin(marks.pixel)
+    own, other = turned_pair(r.turned_pixel, r.landed_pixel)
+    pixel_total = r.total.at[pl.ds(0, pix)]
+
+    for part in range(2):
+        slot = fetched(number)
+        if part == 0:
+            number = fetch(CROSS_V)
+
+        def emit_pixel(columns, value):
+            if part == 0:
+                pixel_total[:, columns] = value
+            else:
+                pixel_total[:, columns] += value
+
+        times_back(r.pair_grad.at[:, pl.ds(part * width, width)], slot, emit_pixel)
+        from_twin(pair_marks[part])
+        n += 1
+        weight_grad(n, own, other, r.pair_grad, r.landed_pair, part * width)
+        reduce.stage(n, 0)
+        if part == 1:
+            norm_back(lambda rows: r.pixels[rows, :].astype(f32), pixel_total, pix, 0, 1, None)
+            meet_out.step(0)
+        for step in range(1, REDUCE_STAGES):
+            reduce.stage(n - step, step)
+    for k in range(1, REDUCE_STAGES):
+        if k < 5:
+            total = meet_out.step(k)
+            if k == 4:
+                r.vector_share[...] = total
+        reduce.tick(n + k)
+    for k in range(5):
+        total = meet_last.step(k)
+    r.square_sum[...] = total
+    reduce.finish()
+    gather.finish()
+    for copy in twins.values():
+        copy.wait_send()
+
+
+def run_block(latents, pixels, mask, out_grad, panel, down, vectors):
+    f32, bf16 = jnp.float32, jnp.bfloat16
+    lat, width = latents.shape
+    pix = pixels.shape[0]
+    share_rows = panel.shape[0]
+    hidden_parts = down.shape[0] // share_rows
+    wide = hidden_parts * width
+    half = LANES // 2
+    blocks = panel.shape[1] // width
+    chunks = blocks + hidden_parts
+    unit = (share_rows, width)
+    vmem = pltpu.VMEM
+    dma, any_space = pltpu.SemaphoreType.DMA, pl.BlockSpec(memory_space=pl.ANY)
+    in_vmem = pl.BlockSpec(memory_space=pltpu.VMEM)
+    inputs = dict(
+        latents=latents,
+        pixels=pixels,
+        mask=mask,
+        out_grad=out_grad,
+        panel=panel,
+        down=down,
+        vectors=vectors,
+    )
+    outputs = dict(
+        latents_out=((lat, width), bf16),
+        latents_grad=((lat, width), f32),
+        panel_share=(panel.shape, f32),
+        down_share=(down.shape, f32),
+        vector_share=(vectors.shape, f32),
+        square_sum=((8, LANES), f32),
+        whole_panel=(CUT + panel.shape, bf16),
+        whole_down=(CUT + down.shape, bf16),
+    )
+    groups = width // LANES
+    lines = -(-RING // 3)
+    scratch = dict(
+        low_panel=vmem(panel.shape, bf16),
+        low_down=vmem(down.shape, bf16),
+        weights=vmem((2, width, width), bf16),
+        rows=vmem((vectors.shape[0] // groups, width), f32),
+        pixel_low=vmem((pix, width), bf16),
+        left=vmem((lat, width), bf16),
+        mixed=vmem((lat, width), bf16),
+        cross_query=vmem((lat, width), bf16),
+        pair=vmem((pix, 2 * width), bf16),
+        first=vmem((lat, width), f32),
+        triple=vmem((lat, 3 * width), bf16),
+        second=vmem((lat, width), f32),
+        hidden=vmem((lat, wide), bf16),
+        slope=vmem((lat, wide), f32),
+        total=vmem((lat, width), f32),
+        grad_low=vmem((lat, width), bf16),
+        cross_low=vmem((lat, width), bf16),
+        triple_grad=vmem((lat, 3 * width), bf16),
+        query_grad=vmem((lat, width), bf16),
+        pair_grad=vmem((pix, 2 * width), bf16),
+        vector_grad=vmem(vectors.shape, f32),
+        squares=vmem((8, LANES), f32),
+        turned_pixel=vmem((2, groups, half, pix), bf16),
+        landed_pixel=vmem((groups, half, pix), bf16),
+        turned_hidden=vmem((2, wide // LANES // 2, hidden_parts, share_rows, lat), bf16),
+        landed_hidden=vmem((wide // LANES // 2, hidden_parts, share_rows, lat), bf16),
+        landed_dz=vmem((lat, width), bf16),
+        landed_du=vmem((lat, wide), bf16),
+        landed_ds=vmem((lat, width), bf16),
+        landed_triple=vmem((lat, 3 * width), bf16),
+        landed_dc=vmem((lat, width), bf16),
+        landed_query=vmem((lat, width), bf16),
+        landed_pair=vmem((pix, 2 * width), bf16),
+        staged=vmem((STAGED, LONG, SHORT, SHORT) + unit, bf16),
+        from_far=vmem((RING, LONG, SHORT) + unit, bf16),
+        from_near_line=vmem((lines, LONG) + unit, bf16),
+        from_near=vmem((RING - lines,) + unit, bf16),
+        from_line_short=vmem((lines, 2 * (LONG - 1)) + unit, bf16),
+        from_line=vmem((RING - lines, 2 * (LONG - 1), SHORT) + unit, bf16),
+        own=dma((chunks,)),
+        load=dma((2,)),
+        gather_send=dma((chunks, GATHER_KINDS)),
+        gather_receive=dma((chunks, GATHER_KINDS)),
+        reduce_send=dma((chunks, REDUCE_KINDS)),
+        reduce_receive=dma((chunks, REDUCE_KINDS)),
+        twin_send=dma((16 + hidden_parts,)),
+        twin_receive=dma((16 + hidden_parts,)),
+        credit=pltpu.SemaphoreType.REGULAR((chunks - RING, 4)),
+    )
+    for name in ("cross", "cross_mix", "self", "self_mix", "feed"):
+        scratch["turned_" + name] = vmem((2, groups, half, lat), bf16)
+        scratch["landed_" + name] = vmem((groups, half, lat), bf16)
+    for name, shape in (("meet", vectors.shape), ("sum", vectors.shape), ("last", (8, LANES))):
+        scratch[name + "_line"] = vmem((LONG,) + shape, f32)
+        scratch[name + "_pairs"] = vmem((6,) + shape, f32)
+        scratch[name + "_send"] = dma((LONG + 2,))
+        scratch[name + "_receive"] = dma((LONG + 2,))
+    names = tuple(inputs) + tuple(outputs) + tuple(scratch)
+    sizes = (width, lat, pix, hidden_parts)
+    results = pl.pallas_call(
+        functools.partial(block_kernel, names, sizes),
+        out_shape=[jax.ShapeDtypeStruct(*spec) for spec in outputs.values()],
+        in_specs=[in_vmem] * len(inputs),
+        out_specs=[in_vmem] * 6 + [any_space] * 2,
+        scratch_shapes=list(scratch.values()),
+        compiler_params=pltpu.CompilerParams(
+            collective_id=0, has_side_effects=True, vmem_limit_bytes=VMEM_LIMIT
+        ),
+    )(*inputs.values())
+    return results[:6]
+
+
+def fast_step(
+    latents,
+    pixels,
+    visible,
+    out_grad,
+    panel,
+    panel_moment,
+    panel_square,
+    down,
+    down_moment,
+    down_square,
+    vectors,
+    vector_moment,
+    vector_square,
+):
+    latent_count, model_width = latents.shape[1:]
+    pixel_count = pixels.shape[1]
+    device_total = lax.axis_size(("dp", "fsdp"))
+    own_start = lax.axis_index(("dp", "fsdp")) * vectors.shape[0]
+    vector_total = vectors.shape[0] * device_total
+    own_vectors = lax.dynamic_update_slice(
+        jnp.zeros((vector_total,), jnp.float32), vectors, (own_start,)
+    )
+    mask = jnp.arange(pixel_count, dtype=jnp.int32)[None, :] < visible[:, None]
+    mask = jnp.broadcast_to(mask.astype(jnp.float32), (8, pixel_count))
+    latents_out, latents_grad, panel_share, down_share, vector_sum, squares = run_block(
+        latents.reshape(-1, model_width),
+        pixels.reshape(-1, model_width),
+        mask,
+        out_grad.reshape(-1, model_width),
+        panel,
+        down,
+        own_vectors.reshape(-1, LANES),
+    )
+    grad_norm = jnp.sqrt(jnp.sum(squares) + jnp.sum(vector_sum * vector_sum))
+    vector_share = lax.dynamic_slice(vector_sum.reshape(-1), (own_start,), vectors.shape)
+    token_total = latents.shape[0] * latent_count * device_total
+    param_total = device_total * (panel.size + down.size + vectors.size)
+    threshold = clip_coeff * (token_total * param_total) ** 0.5
+    factor = threshold / jnp.maximum(grad_norm, threshold)
+    return (
+        latents_out.reshape(latents.shape),
+        latents_grad.reshape(latents.shape),
+        grad_norm,
+        *adam_update(
+            panel, panel_moment, panel_square, panel_share * factor, rate_matrix, weight_decay
+        ),
+        *adam_update(down, down_moment, down_square, down_share * factor, rate_matrix, weight_decay),
+        *adam_update(vectors, vector_moment, vector_square, vector_share * factor, rate_vector, 0.0),
+    )
+
+
+def slow_gather(panel, down, vectors):
+    model_width = panel.shape[1] // 12
+    bf16 = jnp.bfloat16
+    parts = [panel[:, k * 4 * model_width : (k + 1) * 4 * model_width].astype(bf16) for k in range(3)]
+    parts += [down.astype(bf16), vectors.astype(bf16)]
+    return [lax.all_gather(part, ("dp", "fsdp"), axis=0, tiled=True) for part in parts]
+
+
+def slow_reduce(pieces, down_grad, vector_grad, share_length):
+    shares = [
+        lax.psum_scatter(grad, ("dp", "fsdp"), scatter_dimension=0, tiled=True)
+        for grad in (jnp.concatenate(pieces, axis=1), down_grad, vector_grad)
+    ]
+    squares = lax.psum(sum(jnp.sum(share * share) for share in shares), ("dp", "fsdp"))
+    return (*shares, squares)
+
+
 def shards(
+    gather,
+    reduce,
     latents,
     pixels,
     visible,
@@ -165,11 +1338,7 @@
     images, latent_count, model_width = latents.shape
     pixel_count = pixels.shape[1]
     bf16 = jnp.bfloat16
-    full_panel, full_down, full_vector = (
-        lax.all_gather(panel.astype(bf16), ("dp", "fsdp"), axis=0, tiled=True),
-        lax.all_gather(down.astype(bf16), ("dp", "fsdp"), axis=0, tiled=True),
-        lax.all_gather(vectors.astype(bf16), ("dp", "fsdp"), axis=0, tiled=True),
-    )
+    cross_columns, self_columns, up_columns, full_down, full_vector = gather(panel, down, vectors)
     vector_float = full_vector.astype(jnp.float32)
     gain_pixel = vector_slot(vector_float, 0, model_width)
     shift_pixel = vector_slot(vector_float, 1, model_width)
@@ -187,8 +1356,8 @@
     pixel_low = pixel_out.astype(bf16)
     cross_out, cross_normed, cross_inverse = norm_forward(latent_rows, gain_cross, shift_cross)
     cross_low = cross_out.astype(bf16)
-    cross_queries = matmul_low(cross_low, full_panel[:, :model_width]).astype(bf16)
-    pair_rows = matmul_low(pixel_low, full_panel[:, model_width : 3 * model_width]).astype(bf16)
+    cross_queries = matmul_low(cross_low, cross_columns[:, :model_width]).astype(bf16)
+    pair_rows = matmul_low(pixel_low, cross_columns[:, model_width : 3 * model_width]).astype(bf16)
     visible_mask = jnp.arange(pixel_count, dtype=jnp.int32)[None, :] < visible[:, None]
     query_heads = to_heads(cross_queries, images, HEADS)
     key_heads = to_heads(pair_rows[:, :model_width], images, HEADS)
@@ -198,14 +1367,13 @@
     )
     cross_mixed = cross_mix.reshape(-1, model_width)
     first_sum = latent_rows + matmul_low(
-        cross_mixed, full_panel[:, 3 * model_width : 4 * model_width]
-    )
-    self_columns = full_panel[:, 4 * model_width : 8 * model_width]
+        cross_mixed, cross_columns[:, 3 * model_width :]
+    )
     forward_saved = self_forward(first_sum, self_columns, gain_self, shift_self, images)
     second_sum = first_sum + matmul_low(forward_saved[6], self_columns[:, 3 * model_width :])
     feed_out, feed_normed, feed_inverse = norm_forward(second_sum, gain_feed, shift_feed)
     feed_low = feed_out.astype(bf16)
-    upper_in = matmul_low(feed_low, full_panel[:, 8 * model_width :]) + bias_up
+    upper_in = matmul_low(feed_low, up_columns) + bias_up
     hidden_float, gelu_back = jax.vjp(gelu_exact, upper_in)
     hidden = hidden_float.astype(bf16)
     result = second_sum + (matmul_low(hidden, full_down) + bias_down)
@@ -218,15 +1386,12 @@
     grad_up = rows_inner(feed_low, grad_upper)
     grad_bias_up = jnp.sum(grad_upper.astype(jnp.float32), axis=0)
     grad_feed, grad_gain_feed, grad_shift_feed = norm_backward(
-        times_transposed(grad_upper, full_panel[:, 8 * model_width :]),
+        times_transposed(grad_upper, up_columns),
         feed_normed,
         feed_inverse,
         gain_feed,
     )
     grad_two = grad_three + grad_feed
-    again_columns = lax.all_gather(
-        panel[:, 4 * model_width : 8 * model_width].astype(bf16), ("dp", "fsdp"), axis=0, tiled=True
-    )
     (
         self_normed,
         self_inverse,
@@ -237,10 +1402,10 @@
         self_mixed,
         self_top,
         self_total,
-    ) = self_forward(first_sum, again_columns, gain_self, shift_self, images)
+    ) = forward_saved
     grad_self_branch = grad_two.astype(bf16)
     grad_self_out = rows_inner(self_mixed, grad_self_branch)
-    grad_self_mix = times_transposed(grad_self_branch, again_columns[:, 3 * model_width :]).astype(
+    grad_self_mix = times_transposed(grad_self_branch, self_columns[:, 3 * model_width :]).astype(
         bf16
     )
     grad_query_heads, grad_key_heads, grad_value_heads = attend_backward(
@@ -262,17 +1427,16 @@
     ).astype(bf16)
     grad_self_in = rows_inner(self_low, grad_triple)
     grad_first, grad_gain_self, grad_shift_self = norm_backward(
-        times_transposed(grad_triple, again_columns[:, : 3 * model_width]),
+        times_transposed(grad_triple, self_columns[:, : 3 * model_width]),
         self_normed,
         self_inverse,
         gain_self,
     )
     grad_one = grad_two + grad_first
-    self_block = jnp.concatenate([grad_self_in, grad_self_out], axis=1)
     grad_cross_branch = grad_one.astype(bf16)
     grad_cross_out = rows_inner(cross_mixed, grad_cross_branch)
     grad_cross_mix = times_transposed(
-        grad_cross_branch, full_panel[:, 3 * model_width : 4 * model_width]
+        grad_cross_branch, cross_columns[:, 3 * model_width :]
     ).astype(bf16)
     cross_query_grad, cross_key_grad, cross_value_grad = attend_backward(
         to_heads(grad_cross_mix, images, HEADS),
@@ -290,13 +1454,13 @@
     grad_cross_query = rows_inner(cross_low, grad_queries)
     grad_cross_pair = rows_inner(pixel_low, grad_pair)
     grad_input_norm, grad_gain_cross, grad_shift_cross = norm_backward(
-        times_transposed(grad_queries, full_panel[:, :model_width]),
+        times_transposed(grad_queries, cross_columns[:, :model_width]),
         cross_normed,
         cross_inverse,
         gain_cross,
     )
     pixel_unused, grad_gain_pixel, grad_shift_pixel = norm_backward(
-        times_transposed(grad_pair, full_panel[:, model_width : 3 * model_width]),
+        times_transposed(grad_pair, cross_columns[:, model_width : 3 * model_width]),
         pixel_normed,
         pixel_inverse,
         gain_pixel,
@@ -316,25 +1480,22 @@
             grad_bias_up,
         ]
     )
-    cross_block = jnp.concatenate([grad_cross_query, grad_cross_pair, grad_cross_out], axis=1)
-    cross_share, self_share, up_share, down_share, vector_share = (
-        lax.psum_scatter(cross_block, ("dp", "fsdp"), scatter_dimension=0, tiled=True),
-        lax.psum_scatter(self_block, ("dp", "fsdp"), scatter_dimension=0, tiled=True),
-        lax.psum_scatter(grad_up, ("dp", "fsdp"), scatter_dimension=0, tiled=True),
-        lax.psum_scatter(grad_down, ("dp", "fsdp"), scatter_dimension=0, tiled=True),
-        lax.psum_scatter(vector_grad, ("dp", "fsdp"), scatter_dimension=0, tiled=True),
-    )
-    panel_share = jnp.concatenate([cross_share, self_share, up_share], axis=1)
-    local_squares = (
-        jnp.sum(panel_share * panel_share)
-        + jnp.sum(down_share * down_share)
-        + jnp.sum(vector_share * vector_share)
-    )
-    grad_norm = jnp.sqrt(lax.psum(local_squares, ("dp", "fsdp")))
+    pieces = [
+        grad_cross_query,
+        grad_cross_pair,
+        grad_cross_out,
+        grad_self_in,
+        grad_self_out,
+        grad_up,
+    ]
+    panel_share, down_share, vector_share, squares = reduce(
+        pieces, grad_down, vector_grad, vectors.shape[0]
+    )
+    grad_norm = jnp.sqrt(squares)
     device_total = lax.axis_size(("dp", "fsdp"))
     token_total = images * latent_count * device_total
     param_total = (
-        model_width * full_panel.shape[1] + full_down.shape[0] * model_width + full_vector.shape[0]
+        model_width * panel.shape[1] + full_down.shape[0] * model_width + full_vector.shape[0]
     )
     threshold = clip_coeff * (token_total * param_total) ** 0.5
     factor = threshold / jnp.maximum(grad_norm, threshold)
@@ -379,8 +1540,10 @@
         P(("dp", "fsdp")),
         P(("dp", "fsdp")),
     )
+    fast = (mesh.shape["dp"], mesh.shape["fsdp"]) == (LONG * SHORT * SHORT, SHORT)
+    step = fast_step if fast else functools.partial(shards, slow_gather, slow_reduce)
     return jax.shard_map(
-        shards,
+        step,
         mesh=mesh,
         in_specs=placed,
         out_specs=(

time: 1900 us -> 340 us (0.18)
  waiting for transfers between devices: 1570 us -> 0 us
  Pallas kernels: 0 us -> 320 us
  blocking collectives: 126 us -> 0 us
  matrix products: 119 us -> 0 us
  other arithmetic: 31.6 us -> 11.2 us
  local copies, waits for them, and re-layouts: 24.1 us -> 4.51 us
    reduce_scatter x4 -> x0, waiting for transfers between devices: 1340 us -> none  [the longest x1 360 us: shards(): lax.psum_scatter(grad_up, ('dp', 'fsdp'), scatter_dimension=0, tiled=True)]
    pallas_call x0 -> x1, Pallas kernels: none -> 320 us  [run_block(): pl.pallas_call(functools.partial(block_kernel, names, sizes), out_shape=[...]
    all_gather x3 -> x0, waiting for transfers between devices: 224 us -> none  [the longest x1 112 us: shards(): lax.all_gather(panel.astype(bf16), ('dp', 'fsdp'), axis=0, tiled=True)]
    dot_general x33 -> x0, matrix products: 112 us -> none  [the longest x8 42.8 us: matmul_low(): return jnp.dot(left, right, preferred_element_type=jnp.float32)]
    unnamed x2 -> x0, blocking collectives: 85.3 us -> none
    psum x1 -> x0, blocking collectives: 40.4 us -> none  [shards(): grad_norm = jnp.sqrt(lax.psum(local_squares, ('dp', 'fsdp')))]
  transfers between devices with their start and end apart: 7 -> 0, of which waited for: 7 -> 0; matrix products, arithmetic and copies ran while one was open for 5% -> 0% of each run, Pallas kernels for 0% -> 0%
where the time goes in v2:
time: 340 us; the launch traced here: 339 us
  Pallas kernels  320 us (94%)
  other arithmetic  11.2 us (3%)
  local copies, waits for them, and re-layouts  4.51 us (1%)
  between operations  3.91 us (1%)
    pallas_call x1, Pallas kernels, run_block(): pl.pallas_call(functools.partial(block_kernel, names, sizes), out_shape=[...  320 us
    sub x3, other arithmetic, adam_update(): weight - rate * (fixed_moment / (jnp.sqrt(fixed_square) + adam_eps) + dec...  8.48 us

profile of v2, /device:TPU:0, one launch (start us, length us, event | category | flops | bytes accessed | tf_op | source)
XLA Modules:
  0.0 339.4 jit_solution(5750207294207582931)
XLA Ops:
  1.3 0.6 broadcast_in_dim.4.refs_2_
  1.9 0.9 dynamic_update_slice.3
  2.8 0.0 copy-start.8
  2.8 0.6 copy-done.8
  3.4 0.0 copy-start.9
  3.4 0.0 copy-start.10
  3.4 0.0 copy-start.11
  3.4 0.0 copy-start.1
  3.4 0.0 copy-start.6
  3.4 0.0 copy-start.7
  3.4 0.0 copy-start.3
  3.4 319.8 %shard_map.220 = (bf16[256,1024]{1,0:T(8,128)(2,1)}, f32[256,1024]{1,0:T(8,128)}, f32[32,12288]{1,0:T(8,128)}, f32[128,1024]{1,0:T(8,128)}, f32[104,128]{1,0:T(8...) custom-call(bf16[256,1024]{1,0:T(8,128)(2,1)} %bitcast.11, ...), custom_call_target="tpu_custom_call" | custom-call | tf_op jit(solution)/shard_map/pallas_call | solution.py:1239
  323.2 1.4 multiply_reduce_fusion
  324.7 1.3 reduce_sum.18
  327.3 0.0 copy-done.9
  327.3 0.0 copy-done.10
  327.3 0.0 copy-done.11
  327.4 1.4 multiply_subtract_fusion.2
  328.7 0.0 copy-done.1
  328.7 0.0 copy-done.6
  328.7 0.0 copy-done.7
  328.7 0.0 copy-start
  328.8 0.0 copy-start.2
  328.8 2.6 multiply_subtract_fusion.1
  331.4 0.0 copy-done.3
  331.4 0.0 copy-done
  331.4 0.0 copy-done.2
  331.4 0.0 copy-start.5
  331.4 4.5 %multiply_subtract_fusion = (f32[32,12288]{1,0:T(8,128)}, f32[32,12288]{1,0:T(8,128)}, f32[32,12288]{1,0:T(8,128)}) fusion(f32[32,12288]{1,0:T(8,128)S(1)} %copy-done, f32[32,12288]{1,0:T(8,128)} %get-tuple-element.22, f32[]{:T(128)S(6)} %div.48, f32[32,12288]{1,0:T(8,128)S(1)} %copy-done.2, f32[32,12288]{1,0:T(8,128)S(1)} %copy-done.3), kind=kLoop, calls=%fused_computation.2 | loop fusion | flops 6291456 | bytes 11010052 | tf_op jit(solution)/shard_map/sub | solution.py:150
  335.9 0.0 copy-start.4
  335.9 0.0 copy-done.5
  335.9 0.8 copy.29
  336.7 0.6 copy-done.4
  337.3 1.0 copy.30
  (2 shorter events, 0.0 us)
Async XLA Ops:
  2.8 0.6 copy-start.8
  3.4 323.9 %copy-start.9 = (f32[416]{0:T(512)S(1)}, f32[416]{0:T(512)}, u32[]{:S(2)}) copy-start(f32[416]{0:T(512)} %param.23) | copy-start | bytes 4996
  3.4 323.9 %copy-start.10 = (f32[416]{0:T(512)S(1)}, f32[416]{0:T(512)}, u32[]{:S(2)}) copy-start(f32[416]{0:T(512)} %param.24) | copy-start | bytes 4996
  3.4 324.0 %copy-start.11 = (f32[416]{0:T(512)S(1)}, f32[416]{0:T(512)}, u32[]{:S(2)}) copy-start(f32[416]{0:T(512)} %param.25) | copy-start | bytes 4996
  3.4 325.3 %copy-start.1 = (f32[128,1024]{1,0:T(8,128)S(1)}, f32[128,1024]{1,0:T(8,128)}, u32[]{:S(2)}) copy-start(f32[128,1024]{1,0:T(8,128)} %refs_5_.1) | copy-start | bytes 1572868
  3.4 325.3 %copy-start.6 = (f32[128,1024]{1,0:T(8,128)S(1)}, f32[128,1024]{1,0:T(8,128)}, u32[]{:S(2)}) copy-start(f32[128,1024]{1,0:T(8,128)} %param.21) | copy-start | bytes 1572868
  3.4 325.3 %copy-start.7 = (f32[128,1024]{1,0:T(8,128)S(1)}, f32[128,1024]{1,0:T(8,128)}, u32[]{:S(2)}) copy-start(f32[128,1024]{1,0:T(8,128)} %param.22) | copy-start | bytes 1572868
  3.4 328.0 %copy-start.3 = (f32[32,12288]{1,0:T(8,128)S(1)}, f32[32,12288]{1,0:T(8,128)}, u32[]{:S(2)}) copy-start(f32[32,12288]{1,0:T(8,128)} %param.19) | copy-start | bytes 4718596
  328.7 2.6 copy-start
  328.8 2.6 copy-start.2
  331.4 4.5 %copy-start.5 = (bf16[256,1024]{1,0:T(8,128)(2,1)S(1)}, bf16[256,1024]{1,0:T(8,128)(2,1)}, u32[]{:S(2)}) copy-start(bf16[256,1024]{1,0:T(8,128)(2,1)} %get-tuple-element.18) | copy-start | bytes 1572868
  335.9 1.4 copy-start.4

commit v3 on v2

--- a/solution.py
+++ b/solution.py
@@ -156,6 +156,7 @@
 MESH = pl.DeviceIdType.MESH
 LONG, SHORT = 4, 2
 CUT = (LONG, SHORT, SHORT, SHORT)
+PLANE = SHORT * SHORT * SHORT
 VMEM_LIMIT = 60 * 1024 * 1024
 
 
@@ -180,23 +181,22 @@
     def along(self, step):
         return self.device((self.z + step) % LONG, self.x, self.core, self.y)
 
-    def greet(self, everyone_along=False):
+    def across(self, away):
+        flip_x, flip_core, flip_y = away // 4, away // 2 % 2, away % 2
+        return self.device(
+            self.z,
+            1 - self.x if flip_x else self.x,
+            1 - self.core if flip_core else self.core,
+            1 - self.y if flip_y else self.y,
+        )
+
+    def greet(self):
         barrier = pltpu.get_barrier_semaphore()
-
-        def signal(partner):
+        partners = [self.along(step) for step in range(1, LONG)]
+        partners += [self.across(away) for away in range(1, PLANE)]
+        for partner in partners:
             pl.semaphore_signal(barrier, inc=1, device_id=partner, device_id_type=MESH)
-
-        for partner in (self.near_device, self.far_device, self.twin_device):
-            signal(partner)
-        if everyone_along:
-            for step in range(1, LONG):
-                signal(self.along(step))
-            pl.semaphore_wait(barrier, 3 + LONG - 1)
-            return
-        pl.when(self.z < LONG - 1)(lambda: signal(self.up_device))
-        pl.when(self.z > 0)(lambda: signal(self.down_device))
-        at_end = jnp.logical_or(self.z == 0, self.z == LONG - 1)
-        pl.semaphore_wait(barrier, 3 + jnp.where(at_end, 1, 2))
+        pl.semaphore_wait(barrier, len(partners))
 
 
 def remote(source, target, send, receive, device):
@@ -212,6 +212,8 @@
 
 GATHER_KINDS = 4 * (LONG - 1) + 4 + 1 + 2
 GATHER_STAGES = 6
+SPLIT = 2
+SPREAD = 2
 START, RECEIVE, SENT = range(3)
 
 
@@ -520,9 +522,10 @@
 
 
 class Meeting:
-    def __init__(self, here, value, line, pairs, send, receive):
-        self.here, self.value, self.line, self.pairs = here, value, line, pairs
+    def __init__(self, here, value, line, plane, send, receive):
+        self.here, self.value, self.line, self.plane = here, value, line, plane
         self.send, self.receive = send, receive
+        self.place = here.x * 4 + here.core * 2 + here.y
 
     def along(self, step, back=False):
         here = self.here
@@ -535,15 +538,18 @@
             here.along(step),
         )
 
-    def pair(self, k):
+    def across(self, away, back=False):
         here = self.here
-        device = (here.near_device, here.far_device, here.twin_device)[k]
+        place = self.place
+        if back:
+            x = 1 - here.x if away // 4 else here.x
+            core = 1 - here.core if away // 2 % 2 else here.core
+            y = 1 - here.y if away % 2 else here.y
+            place = x * 4 + core * 2 + y
+        block = self.plane.at[place]
+        number = LONG - 2 + away
         return remote(
-            self.pairs.at[2 * k],
-            self.pairs.at[2 * k + 1],
-            self.send.at[LONG - 1 + k],
-            self.receive.at[LONG - 1 + k],
-            device,
+            block, block, self.send.at[number], self.receive.at[number], here.across(away)
         )
 
     def step(self, k):
@@ -559,17 +565,24 @@
             total = self.line[0]
             for place in range(1, LONG):
                 total = total + self.line[place]
-        else:
-            self.pair(k - 2).wait()
-            total = self.pairs[2 * k - 4] + self.pairs[2 * k - 3]
-        if k < 4:
-            self.pairs[2 * k - 2] = total
-            self.pair(k - 1).start()
+            self.plane[self.place] = total
+            for away in range(1, PLANE):
+                self.across(away).start()
+            return None
+        for away in range(1, PLANE):
+            self.across(away).wait_send()
+            self.across(away, True).wait_recv()
+        total = self.plane[0]
+        for place in range(1, PLANE):
+            total = total + self.plane[place]
         return total
 
 
 TILE = 256
 LANES = 128
+FORWARD_BUDGET = 1.5
+VECTOR_TICKS = (0, 7, 9)
+TURNED, LANDED = "turned_", "landed_"
 BAND = 32
 CROSS_Q, CROSS_K, CROSS_V, CROSS_O, SELF_Q, SELF_K, SELF_V, SELF_O, UP = range(9)
 
@@ -579,7 +592,7 @@
 
 
 def bands(rows, body, carry=0):
-    return lax.fori_loop(0, rows // BAND, lambda k, c: body(tile(k * BAND, BAND), c), carry)
+    return lax.fori_loop(0, rows // BAND, lambda k, c: body(tile(k * BAND, BAND), c), carry, unroll=4)
 
 
 def normalised(values):
@@ -590,7 +603,7 @@
 
 def block_kernel(names, sizes, *refs):
     r = types.SimpleNamespace(**dict(zip(names, refs, strict=True)))
-    width, lat, pix, hidden_parts = sizes
+    width, lat, pix, hidden_parts, threshold = sizes
     f32, bf16 = jnp.float32, jnp.bfloat16
     here = Place()
     core = here.core
@@ -600,35 +613,39 @@
     gather_order += list(range(UP, panel_blocks))
     share_rows = r.panel.shape[0]
 
-    meet_in = Meeting(here, r.vectors, r.meet_line, r.meet_pairs, r.meet_send, r.meet_receive)
-    meet_out = Meeting(here, r.vector_grad, r.sum_line, r.sum_pairs, r.sum_send, r.sum_receive)
-    meet_last = Meeting(here, r.squares, r.last_line, r.last_pairs, r.last_send, r.last_receive)
+    meet_in = Meeting(here, r.vectors, r.meet_line, r.meet_plane, r.meet_send, r.meet_receive)
+    meet_out = Meeting(here, r.vector_grad, r.sum_line, r.sum_plane, r.sum_send, r.sum_receive)
+    meet_last = Meeting(here, r.squares, r.last_line, r.last_plane, r.last_send, r.last_receive)
 
     chunks, keep = [], []
+
+    def keep_own(low, whole):
+        own = whole.at[here.z, here.x, core, here.y]
+        keep.append(pltpu.make_async_copy(low, own, r.own.at[len(keep)]))
+        keep[-1].start()
+
     for block in gather_order:
         columns = pl.ds(block * width, width)
         r.low_panel[:, columns] = r.panel[:, columns].astype(bf16)
-        whole = r.whole_panel.at[:, :, :, :, :, columns]
-        chunks.append(whole)
-        own = whole.at[here.z, here.x, core, here.y]
-        keep.append(pltpu.make_async_copy(r.low_panel.at[:, columns], own, r.own.at[len(keep)]))
-        keep[-1].start()
-    for part in range(hidden_parts):
-        rows = pl.ds(part * share_rows, share_rows)
+        keep_own(r.low_panel.at[:, columns], r.whole_panel.at[:, :, :, :, :, columns])
+        for part in range(SPLIT):
+            columns = pl.ds(block * width + part * width // SPLIT, width // SPLIT)
+            chunks.append(r.whole_panel.at[:, :, :, :, :, columns])
+    for block in range(hidden_parts):
+        rows = pl.ds(block * share_rows, share_rows)
         r.low_down[rows, :] = r.down[rows, :].astype(bf16)
-        whole = r.whole_down.at[:, :, :, :, rows]
-        chunks.append(whole)
-        own = whole.at[here.z, here.x, core, here.y]
-        keep.append(pltpu.make_async_copy(r.low_down.at[rows], own, r.own.at[len(keep)]))
-        keep[-1].start()
+        keep_own(r.low_down.at[rows], r.whole_down.at[:, :, :, :, rows])
+        for part in range(SPLIT):
+            rows = pl.ds(block * share_rows + part * share_rows // SPLIT, share_rows // SPLIT)
+            chunks.append(r.whole_down.at[:, :, :, :, rows])
     gather = Gather(here, chunks, r.gather_send, r.gather_receive)
-    here.greet(True)
+    here.greet()
 
     def gather_tick(tick):
-        if tick < len(keep):
-            keep[tick].wait()
+        if tick % SPLIT == 0 and tick < len(chunks):
+            keep[tick // SPLIT].wait()
         for step in range(GATHER_STAGES):
-            gather.stage(tick - step, step)
+            gather.stage(tick - SPREAD * step, step)
 
     twins = {}
 
@@ -689,7 +706,7 @@
             emit(columns, jnp.dot(left[...], r.weights[slot, :, columns], preferred_element_type=f32))
             return carry
 
-        lax.fori_loop(0, width // TILE, one, 0)
+        lax.fori_loop(0, width // TILE, one, 0, unroll=4)
 
     def times_back(left, slot, emit):
         def one(k, carry):
@@ -697,7 +714,7 @@
             emit(columns, times_transposed(left[...], r.weights[slot, columns, :]))
             return carry
 
-        lax.fori_loop(0, width // TILE, one, 0)
+        lax.fori_loop(0, width // TILE, one, 0, unroll=4)
 
     def norm_rows(read, count, gain, shift, target):
         def one(rows, carry):
@@ -750,7 +767,7 @@
         powers = jnp.exp(scores - jnp.max(scores, axis=-1, keepdims=True))
         return powers / jnp.sum(powers, axis=-1, keepdims=True)
 
-    def attend(queries, keys, key_start, values, value_start, masked, target):
+    def attend(heads, queries, keys, key_start, values, value_start, masked, target):
         def one(k, carry):
             columns = tile(k * head, head)
             probability = probabilities(
@@ -760,7 +777,7 @@
             target[:, columns] = matmul_low(probability.astype(bf16), value_rows).astype(bf16)
             return carry
 
-        lax.fori_loop(0, HEADS, one, 0)
+        lax.fori_loop(*heads, one, 0, unroll=HEADS // 2)
 
     def attend_back(grad, queries, keys, key_start, values, value_start, masked, targets):
         query_grad, key_grad, key_at, value_grad, value_at = targets
@@ -784,7 +801,7 @@
             ).astype(bf16)
             return carry
 
-        lax.fori_loop(0, HEADS, one, 0)
+        lax.fori_loop(0, HEADS, one, 0, unroll=4)
 
     row_id = lax.broadcasted_iota(jnp.int32, (LANES, LANES), 0)
     unit = (row_id == lax.broadcasted_iota(jnp.int32, (LANES, LANES), 1)).astype(bf16)
@@ -796,7 +813,7 @@
                 target[side, k] = turned[side * LANES // 2 : (side + 1) * LANES // 2]
             return carry
 
-        lax.fori_loop(0, width // LANES, one, 0)
+        lax.fori_loop(0, width // LANES, one, 0, unroll=8)
         return to_twin(target.at[1 - core], landing)
 
     def weight_grad(n, own, other, grad, grad_other, start):
@@ -815,7 +832,7 @@
                     r.staged[slot, :, first, second, :, into] = total[:, to_x, to_y]
             return carry
 
-        lax.fori_loop(0, width // TILE, one, 0)
+        lax.fori_loop(0, width // TILE, one, 0, unroll=4)
 
     def turned_pair(target, landing):
         rows = target.shape[3]
@@ -824,19 +841,24 @@
             lambda: landing[...].reshape(-1, rows),
         )
 
-    dz_sent = None
     marks = types.SimpleNamespace()
 
-    def after_vectors(total):
+    def set_rows(total):
         per = width // LANES
         for row in range(r.rows.shape[0]):
             for at in range(per):
                 line = total[row * per + at : row * per + at + 1, :]
                 r.rows[row : row + 1, at * LANES : (at + 1) * LANES] = line.astype(bf16).astype(f32)
-        norm_rows(lambda rows: r.pixels[rows, :].astype(f32), pix, 0, 1, r.pixel_low)
-        norm_rows(lambda rows: r.latents[rows, :].astype(f32), lat, 2, 3, r.left)
-        marks.pixel = turn(r.pixel_low, r.turned_pixel, r.landed_pixel)
-        marks.cross = turn(r.left, r.turned_cross, r.landed_cross)
+
+    def after_vectors():
+        yield 0.5, lambda: norm_rows(
+            lambda rows: r.pixels[rows, :].astype(f32), pix, 0, 1, r.pixel_low
+        )
+        yield 0.9, lambda: norm_rows(
+            lambda rows: r.latents[rows, :].astype(f32), lat, 2, 3, r.left
+        )
+        yield 0.4, lambda: mark_turn("pixel", r.pixel_low)
+        yield 0.5, lambda: mark_turn("cross", r.left)
 
     def to_columns(target, start=0):
         def emit(columns, value):
@@ -851,28 +873,40 @@
 
         return emit
 
-    def forward(block, slot):
-        if block == CROSS_K:
-            times(r.pixel_low, slot, to_columns(r.pair))
-        elif block == CROSS_V:
-            times(r.pixel_low, slot, to_columns(r.pair, width))
+    def mark_turn(name, source):
+        landing = getattr(r, LANDED + name)
+        setattr(marks, name, turn(source, getattr(r, TURNED + name), landing))
+
+    halves = ((0, HEADS // 2), (HEADS // 2, HEADS))
+
+    def forward(block, number):
+        if block in (CROSS_K, CROSS_V):
+            emit = to_columns(r.pair, (block - CROSS_K) * width)
+            yield 0.6, lambda: times(r.pixel_low, fetched(number), emit)
         elif block == CROSS_Q:
-            times(r.left, slot, to_columns(r.cross_query))
-            attend(r.cross_query, r.pair, 0, r.pair, width, True, r.mixed)
-            marks.cross_mix = turn(r.mixed, r.turned_cross_mix, r.landed_cross_mix)
+            yield 0.8, lambda: times(r.left, fetched(number), to_columns(r.cross_query))
+            for heads in halves:
+                yield 1.0, functools.partial(
+                    attend, heads, r.cross_query, r.pair, 0, r.pair, width, True, r.mixed
+                )
+            yield 0.5, lambda: mark_turn("cross_mix", r.mixed)
         elif block == CROSS_O:
-            times(r.mixed, slot, add_columns(r.first, r.latents))
-            norm_rows(lambda rows: r.first[rows, :], lat, 4, 5, r.left)
-            marks.self = turn(r.left, r.turned_self, r.landed_self)
+            yield 0.8, lambda: times(r.mixed, fetched(number), add_columns(r.first, r.latents))
+            yield 0.8, lambda: norm_rows(lambda rows: r.first[rows, :], lat, 4, 5, r.left)
+            yield 0.5, lambda: mark_turn("self", r.left)
         elif block in (SELF_Q, SELF_K, SELF_V):
-            times(r.left, slot, to_columns(r.triple, (block - SELF_Q) * width))
+            emit = to_columns(r.triple, (block - SELF_Q) * width)
+            yield 0.8, lambda: times(r.left, fetched(number), emit)
             if block == SELF_V:
-                attend(r.triple, r.triple, width, r.triple, 2 * width, False, r.mixed)
-                marks.self_mix = turn(r.mixed, r.turned_self_mix, r.landed_self_mix)
+                for heads in halves:
+                    yield 1.5, functools.partial(
+                        attend, heads, r.triple, r.triple, width, r.triple, 2 * width, False, r.mixed
+                    )
+                yield 0.5, lambda: mark_turn("self_mix", r.mixed)
         elif block == SELF_O:
-            times(r.mixed, slot, add_columns(r.second, r.first))
-            norm_rows(lambda rows: r.second[rows, :], lat, 6, 7, r.left)
-            marks.feed = turn(r.left, r.turned_feed, r.landed_feed)
+            yield 0.8, lambda: times(r.mixed, fetched(number), add_columns(r.second, r.first))
+            yield 0.8, lambda: norm_rows(lambda rows: r.second[rows, :], lat, 6, 7, r.left)
+            yield 0.5, lambda: mark_turn("feed", r.left)
         else:
             part = block - UP
 
@@ -884,8 +918,6 @@
                 density = jnp.exp(-0.5 * upper * upper) * ((2.0 * math.pi) ** -0.5)
                 r.slope[:, where] = below + upper * density
 
-            times(r.left, slot, emit)
-
             def one(k, carry):
                 block_at = part * (width // LANES) + k
                 turned = times_transposed(unit, r.hidden[:, tile(block_at * LANES, LANES)])
@@ -894,29 +926,52 @@
                 r.turned_hidden[side, block_at // 4 * 2 + k % 2] = turned
                 return carry
 
-            lax.fori_loop(0, width // LANES, one, 0)
-
-    ticks = len(chunks) + GATHER_STAGES - 1
-    lead = GATHER_STAGES + 1
+            yield 1.5, lambda: times(r.left, fetched(number), emit)
+            yield 0.6, lambda: lax.fori_loop(0, width // LANES, one, 0, unroll=8)
+
     forward_blocks = len(gather_order)
-    for tick in range(forward_blocks + lead):
+    ticks = len(chunks) + SPREAD * (GATHER_STAGES - 1)
+    arrival = SPLIT - 1 + SPREAD * (GATHER_STAGES - 1) + 1
+    todo, taken = [], 0
+
+    def work(budget, until=None):
+        nonlocal taken
+        spent = 0.0
+        while taken < len(todo) and (spent < budget or (until is not None and taken < until)):
+            cost, step = todo[taken]
+            taken += 1
+            step()
+            spent += cost
+
+    tick, fetch_next, ends = 0, 0, []
+    while fetch_next < forward_blocks:
         gather_tick(tick)
-        if tick < 5:
-            total = meet_in.step(tick)
-            if tick == 4:
-                after_vectors(total)
-        elif tick == 5:
+        if tick in VECTOR_TICKS:
+            total = meet_in.step(VECTOR_TICKS.index(tick))
+            if tick == VECTOR_TICKS[2]:
+                set_rows(total)
+                todo.extend(after_vectors())
+        elif tick == VECTOR_TICKS[2] + 1:
             marks.dz = to_twin(r.out_grad, r.landed_dz)
-        if 0 <= tick - lead + 1 < forward_blocks:
-            gather.whole(tick - lead + 1)
-            fetch(gather_order[tick - lead + 1])
-        if tick - lead >= 0:
-            forward(gather_order[tick - lead], fetched(tick - lead))
+        if tick >= SPLIT * fetch_next + arrival:
+            if len(ends) > 1:
+                work(0.0, ends[-2])
+            for n in range(SPLIT * fetch_next, SPLIT * fetch_next + SPLIT):
+                gather.whole(n)
+            number = fetch(gather_order[fetch_next])
+            work(FORWARD_BUDGET)
+            todo.extend(forward(gather_order[fetch_next], number))
+            ends.append(len(todo))
+            fetch_next += 1
+        else:
+            work(FORWARD_BUDGET)
+        tick += 1
+    work(1e9)
     marks.hidden = to_twin(r.turned_hidden.at[1 - core], r.landed_hidden)
 
     r.squares[...] = jnp.zeros_like(r.squares)
-    for tick in range(forward_blocks + lead, ticks):
-        gather_tick(tick)
+    gather_tick(tick)
+    tick += 1
     from_twin(marks.dz)
     from_twin(marks.hidden)
 
@@ -931,11 +986,19 @@
         )
         reduce.tick(part)
 
-    hidden_grad(0)
-    for n in range(forward_blocks, len(chunks)):
+    part = 0
+    while tick < ticks:
+        if part < 3:
+            hidden_grad(part)
+            part += 1
+        for _ in range(2):
+            if tick < ticks:
+                gather_tick(tick)
+                tick += 1
+    hidden_next = part
+    for n in range(SPLIT * forward_blocks, len(chunks)):
         gather.whole(n)
     number = fetch(("down", 0))
-    hidden_grad(1)
 
     def start_out(rows, carry):
         r.total[rows, :] = r.second[rows, :] + vector(8)
@@ -969,8 +1032,8 @@
         slot = fetched(number)
         number = fetch(("down", part + 1) if part + 1 < hidden_parts else UP)
         out_and_du(part, slot)
-        if part + 2 < hidden_parts:
-            hidden_grad(part + 2)
+        if hidden_next + part < hidden_parts:
+            hidden_grad(hidden_next + part)
 
     def finish_out(rows, carry):
         r.latents_out[rows, :] = r.total[rows, :].astype(bf16)
@@ -1127,21 +1190,25 @@
         for step in range(1, REDUCE_STAGES):
             reduce.stage(n - step, step)
     for k in range(1, REDUCE_STAGES):
-        if k < 5:
-            total = meet_out.step(k)
-            if k == 4:
-                r.vector_share[...] = total
+        if k == 1:
+            meet_out.step(1)
+        elif k == 3:
+            total = meet_out.step(2)
+            r.vector_share[...] = total
+            vector_squares = jnp.sum(total * total)
         reduce.tick(n + k)
-    for k in range(5):
+    for k in range(3):
         total = meet_last.step(k)
-    r.square_sum[...] = total
+    norm = jnp.sqrt(jnp.zeros((8, LANES), f32) + (jnp.sum(total) + vector_squares))
+    r.norms[0] = norm
+    r.norms[1] = threshold / jnp.maximum(norm, threshold)
     reduce.finish()
     gather.finish()
     for copy in twins.values():
         copy.wait_send()
 
 
-def run_block(latents, pixels, mask, out_grad, panel, down, vectors):
+def run_block(latents, pixels, mask, out_grad, panel, down, vectors, threshold):
     f32, bf16 = jnp.float32, jnp.bfloat16
     lat, width = latents.shape
     pix = pixels.shape[0]
@@ -1170,7 +1237,7 @@
         panel_share=(panel.shape, f32),
         down_share=(down.shape, f32),
         vector_share=(vectors.shape, f32),
-        square_sum=((8, LANES), f32),
+        norms=((2, 8, LANES), f32),
         whole_panel=(CUT + panel.shape, bf16),
         whole_down=(CUT + down.shape, bf16),
     )
@@ -1218,8 +1285,8 @@
         from_line=vmem((RING - lines, 2 * (LONG - 1), SHORT) + unit, bf16),
         own=dma((chunks,)),
         load=dma((2,)),
-        gather_send=dma((chunks, GATHER_KINDS)),
-        gather_receive=dma((chunks, GATHER_KINDS)),
+        gather_send=dma((chunks * SPLIT, GATHER_KINDS)),
+        gather_receive=dma((chunks * SPLIT, GATHER_KINDS)),
         reduce_send=dma((chunks, REDUCE_KINDS)),
         reduce_receive=dma((chunks, REDUCE_KINDS)),
         twin_send=dma((16 + hidden_parts,)),
@@ -1227,15 +1294,15 @@
         credit=pltpu.SemaphoreType.REGULAR((chunks - RING, 4)),
     )
     for name in ("cross", "cross_mix", "self", "self_mix", "feed"):
-        scratch["turned_" + name] = vmem((2, groups, half, lat), bf16)
-        scratch["landed_" + name] = vmem((groups, half, lat), bf16)
+        scratch[TURNED + name] = vmem((2, groups, half, lat), bf16)
+        scratch[LANDED + name] = vmem((groups, half, lat), bf16)
     for name, shape in (("meet", vectors.shape), ("sum", vectors.shape), ("last", (8, LANES))):
         scratch[name + "_line"] = vmem((LONG,) + shape, f32)
-        scratch[name + "_pairs"] = vmem((6,) + shape, f32)
-        scratch[name + "_send"] = dma((LONG + 2,))
-        scratch[name + "_receive"] = dma((LONG + 2,))
+        scratch[name + "_plane"] = vmem((PLANE,) + shape, f32)
+        scratch[name + "_send"] = dma((LONG + PLANE - 2,))
+        scratch[name + "_receive"] = dma((LONG + PLANE - 2,))
     names = tuple(inputs) + tuple(outputs) + tuple(scratch)
-    sizes = (width, lat, pix, hidden_parts)
+    sizes = (width, lat, pix, hidden_parts, threshold)
     results = pl.pallas_call(
         functools.partial(block_kernel, names, sizes),
         out_shape=[jax.ShapeDtypeStruct(*spec) for spec in outputs.values()],
@@ -1247,6 +1314,42 @@
         ),
     )(*inputs.values())
     return results[:6]
+
+
+ADAM_STEPS = 4
+
+
+def adam_kernel(norms, *refs):
+    factor = norms[1, 0:1, 0:1]
+    ins, outs = refs[:10], refs[10:]
+    for at in range(2):
+        grad, weight, moment, square = ins[4 * at : 4 * at + 4]
+        after = adam_update(
+            weight[...], moment[...], square[...], grad[...] * factor, rate_matrix, weight_decay
+        )
+        for out, value in zip(outs[3 * at : 3 * at + 3], after):
+            out[...] = value
+    for out, value in zip(outs[6:], ins[8:]):
+        out[...] = value[...]
+
+
+def adam_all(norms, panels, downs, passed):
+    columns = panels[0].shape[1] // ADAM_STEPS
+    in_columns = pl.BlockSpec((panels[0].shape[0], columns), lambda k: (0, k))
+
+    def in_rows(array):
+        return pl.BlockSpec((array.shape[0] // ADAM_STEPS, array.shape[1]), lambda k: (k, 0))
+
+    arrays = panels + downs + passed
+    specs = [in_columns] * 4 + [in_rows(array) for array in downs + passed]
+    keep = [1, 2, 3, 5, 6, 7, 8, 9]
+    return pl.pallas_call(
+        adam_kernel,
+        grid=(ADAM_STEPS,),
+        out_shape=[jax.ShapeDtypeStruct(arrays[k].shape, arrays[k].dtype) for k in keep],
+        in_specs=[pl.BlockSpec(norms.shape, lambda k: (0, 0, 0))] + specs,
+        out_specs=[specs[k] for k in keep],
+    )(norms, *arrays)
 
 
 def fast_step(
@@ -1274,7 +1377,10 @@
     )
     mask = jnp.arange(pixel_count, dtype=jnp.int32)[None, :] < visible[:, None]
     mask = jnp.broadcast_to(mask.astype(jnp.float32), (8, pixel_count))
-    latents_out, latents_grad, panel_share, down_share, vector_sum, squares = run_block(
+    token_total = latents.shape[0] * latent_count * device_total
+    param_total = device_total * (panel.size + down.size + vectors.size)
+    threshold = clip_coeff * (token_total * param_total) ** 0.5
+    latents_out, latents_grad, panel_share, down_share, vector_sum, norms = run_block(
         latents.reshape(-1, model_width),
         pixels.reshape(-1, model_width),
         mask,
@@ -1282,21 +1388,21 @@
         panel,
         down,
         own_vectors.reshape(-1, LANES),
-    )
-    grad_norm = jnp.sqrt(jnp.sum(squares) + jnp.sum(vector_sum * vector_sum))
+        threshold,
+    )
     vector_share = lax.dynamic_slice(vector_sum.reshape(-1), (own_start,), vectors.shape)
-    token_total = latents.shape[0] * latent_count * device_total
-    param_total = device_total * (panel.size + down.size + vectors.size)
-    threshold = clip_coeff * (token_total * param_total) ** 0.5
-    factor = threshold / jnp.maximum(grad_norm, threshold)
+    grad_norm, factor = norms[0, 0, 0], norms[1, 0, 0]
+    *after, latents_grad, latents_out = adam_all(
+        norms,
+        [panel_share, panel, panel_moment, panel_square],
+        [down_share, down, down_moment, down_square],
+        [latents_grad, latents_out],
+    )
     return (
         latents_out.reshape(latents.shape),
         latents_grad.reshape(latents.shape),
         grad_norm,
-        *adam_update(
-            panel, panel_moment, panel_square, panel_share * factor, rate_matrix, weight_decay
-        ),
-        *adam_update(down, down_moment, down_square, down_share * factor, rate_matrix, weight_decay),
+        *after,
         *adam_update(vectors, vector_moment, vector_square, vector_share * factor, rate_vector, 0.0),
     )
 

time: 340 us -> 318 us (0.935); the launches traced: 339 us -> 312 us
  Pallas kernels: 320 us -> 305 us
  other arithmetic: 11.2 us -> 2.03 us
    pallas_call x1, Pallas kernels: 320 us -> 297 us  [run_block(): pl.pallas_call(functools.partial(block_kernel, names, sizes), out_shape=[...]
    pallas_call x0 -> x1, Pallas kernels: none -> 8.17 us  [adam_all(): pl.pallas_call(adam_kernel, grid=(ADAM_STEPS,), out_shape=[jax.ShapeDtype...]
    sub x3 -> x1, other arithmetic: 8.48 us -> 2.03 us  [adam_update(): weight - rate * (fixed_moment / (jnp.sqrt(fixed_square) + adam_eps) + dec...]
where the time goes in v3:
time: 318 us; the launch traced here: 312 us
  Pallas kernels  305 us (96%)
  local copies, waits for them, and re-layouts  3.29 us (1%)
    pallas_call x1, Pallas kernels, run_block(): pl.pallas_call(functools.partial(block_kernel, names, sizes), out_shape=[...  297 us
    pallas_call x1, Pallas kernels, adam_all(): pl.pallas_call(adam_kernel, grid=(ADAM_STEPS,), out_shape=[jax.ShapeDtype...  8.17 us

profile of v3, /device:TPU:0, one launch (start us, length us, event | category | flops | bytes accessed | tf_op | source)
XLA Modules:
  0.0 312.4 jit_solution(14343515659382970456)
XLA Ops:
  1.3 0.6 broadcast_in_dim.4.refs_2_
  1.9 0.9 dynamic_update_slice.3
  2.8 0.0 copy-start
  2.8 0.6 copy-done
  3.4 0.0 copy-start.1
  3.4 0.0 copy-start.2
  3.4 0.0 copy-start.3
  3.4 297.1 %shard_map.220 = (bf16[256,1024]{1,0:T(8,128)(2,1)}, f32[256,1024]{1,0:T(8,128)}, f32[32,12288]{1,0:T(8,128)}, f32[128,1024]{1,0:T(8,128)}, f32[104,128]{1,0:T(8...) custom-call(bf16[256,1024]{1,0:T(8,128)(2,1)} %bitcast.11, ...), custom_call_target="tpu_custom_call" | custom-call | tf_op jit(solution)/shard_map/pallas_call | solution.py:1306
  300.5 1.2 fusion.2
  301.7 0.0 copy-done.1
  301.7 0.0 copy-done.2
  301.7 0.0 copy-done.3
  301.7 2.0 multiply_subtract_fusion
  303.7 8.2 %shard_map.221 = (f32[32,12288]{1,0:T(8,128)}, f32[32,12288]{1,0:T(8,128)}, f32[32,12288]{1,0:T(8,128)}, f32[128,1024]{1,0:T(8,128)}, f32[128,1024]{1,0:T(8,128)...) custom-call(f32[2,8,128]{2,1,0:T(8,128)} %get-tuple-element.26.norms, ...), custom_call_target="tpu_custom_call" | custom-call | tf_op jit(solution)/shard_map/pallas_call | solution.py:1346
  (2 shorter events, 0.0 us)
Async XLA Ops:
  2.8 0.6 copy-start
  3.4 298.3 %copy-start.1 = (f32[416]{0:T(512)S(1)}, f32[416]{0:T(512)}, u32[]{:S(2)}) copy-start(f32[416]{0:T(512)} %param.23) | copy-start | bytes 4996
  3.4 298.3 %copy-start.2 = (f32[416]{0:T(512)S(1)}, f32[416]{0:T(512)}, u32[]{:S(2)}) copy-start(f32[416]{0:T(512)} %param.24) | copy-start | bytes 4996
  3.4 298.3 %copy-start.3 = (f32[416]{0:T(512)S(1)}, f32[416]{0:T(512)}, u32[]{:S(2)}) copy-start(f32[416]{0:T(512)} %param.25) | copy-start | bytes 4996

commit v4 on v3

--- a/solution.py
+++ b/solution.py
@@ -336,6 +336,7 @@
 REDUCE_STAGES = 6
 RING = 9
 STAGED = 3
+DIRECT = 2
 
 
 class Reduce:
@@ -344,6 +345,9 @@
 
     def line_last(self, n):
         return n % 3 == 0
+
+    def direct(self, n):
+        return n >= self.count - DIRECT
 
     def at(self, n):
         slot = n % RING
@@ -361,11 +365,44 @@
     def near(self, n):
         r, here = self.r, self.here
         slot, index = self.at(n)
-        if self.line_last(n):
+        if self.direct(n):
+            source = r.from_far.at[slot, :, 1 - here.first]
+            target = r.direct_near.at[n - self.count + DIRECT]
+        elif self.line_last(n):
             source, target = r.from_far.at[slot, :, 1 - here.first], r.from_near_line.at[index]
         else:
             source, target = r.from_far.at[slot, here.z, 1 - here.first], r.from_near.at[index]
         return self.copy(n, 1, source, target, here.near_device)
+
+    def along(self, n, step):
+        r, here, index = self.r, self.here, n - self.count + DIRECT
+        source = r.direct_near.at[index, (here.z + step) % LONG]
+        return self.copy(n, 1 + step, source, r.direct_line.at[index, step - 1], here.along(step))
+
+    def stage_direct(self, n, step):
+        r, here, index = self.r, self.here, n - self.count + DIRECT
+        slot = n % RING
+        if step == 1:
+            self.credit(n, 1)
+            self.credit(n, 3, here.z < LONG - 1)
+            self.credit(n, 2, here.z > 0)
+            self.near(n).start()
+        elif step == 2:
+            self.near(n).wait_recv()
+
+            def one(at, carry):
+                add_up(r.direct_near.at[index, at], r.from_far.at[slot, at, here.first])
+                return carry
+
+            lax.fori_loop(0, LONG, one, 0)
+            for away in range(1, LONG):
+                self.along(n, away).start()
+        elif step == 3:
+            value = r.direct_near[index, here.z].astype(jnp.float32)
+            for away in range(1, LONG):
+                self.along(n, away).wait_recv()
+                value = value + r.direct_line[index, away - 1].astype(jnp.float32)
+            self.put(n, value)
 
     def line(self, n, place):
         r = self.r
@@ -468,11 +505,15 @@
                 return carry
 
             lax.fori_loop(0, LONG * SHORT, one, 0)
-            if self.line_last(n):
+            if self.direct(n):
+                self.stage_direct(n, step)
+            elif self.line_last(n):
                 self.credit(n, 1)
                 self.near(n).start()
             else:
                 self.first_hop(n)
+        elif self.direct(n):
+            self.stage_direct(n, step)
         elif self.line_last(n):
             if step == 2:
                 self.near(n).wait_recv()
@@ -513,7 +554,10 @@
         for n in range(max(0, self.count - RING), self.count):
             self.near(n).wait_send()
             for step in range(1, LONG):
-                self.hop(n, step, SENT)
+                if self.direct(n):
+                    self.along(n, step).wait_send()
+                else:
+                    self.hop(n, step, SENT)
 
 
 def add_up(target, source):
@@ -1189,10 +1233,10 @@
             meet_out.step(0)
         for step in range(1, REDUCE_STAGES):
             reduce.stage(n - step, step)
-    for k in range(1, REDUCE_STAGES):
+    for k in range(1, REDUCE_STAGES - DIRECT):
         if k == 1:
             meet_out.step(1)
-        elif k == 3:
+        elif k == 2:
             total = meet_out.step(2)
             r.vector_share[...] = total
             vector_squares = jnp.sum(total * total)
@@ -1283,6 +1327,8 @@
         from_near=vmem((RING - lines,) + unit, bf16),
         from_line_short=vmem((lines, 2 * (LONG - 1)) + unit, bf16),
         from_line=vmem((RING - lines, 2 * (LONG - 1), SHORT) + unit, bf16),
+        direct_near=vmem((DIRECT, LONG) + unit, bf16),
+        direct_line=vmem((DIRECT, LONG - 1) + unit, bf16),
         own=dma((chunks,)),
         load=dma((2,)),
         gather_send=dma((chunks * SPLIT, GATHER_KINDS)),

time: 318 us -> 315 us (level)
  no operation moved by 1% of the time
where the time goes in v4:
time: 315 us; the launch traced here: 310 us
  Pallas kernels  302 us (96%)
  local copies, waits for them, and re-layouts  3.29 us (1%)
    pallas_call x1, Pallas kernels, run_block(): pl.pallas_call(functools.partial(block_kernel, names, sizes), out_shape=[...  294 us
    pallas_call x1, Pallas kernels, adam_all(): pl.pallas_call(adam_kernel, grid=(ADAM_STEPS,), out_shape=[jax.ShapeDtype...  8.17 us

profile of v4, /device:TPU:0, one launch (start us, length us, event | category | flops | bytes accessed | tf_op | source)
XLA Modules:
  0.0 309.5 jit_solution(7403382728996164934)
XLA Ops:
  1.3 0.6 broadcast_in_dim.4.refs_2_
  1.9 0.9 dynamic_update_slice.3
  2.8 0.0 copy-start
  2.8 0.6 copy-done
  3.4 0.0 copy-start.1
  3.4 0.0 copy-start.2
  3.4 0.0 copy-start.3
  3.4 294.3 %shard_map.220 = (bf16[256,1024]{1,0:T(8,128)(2,1)}, f32[256,1024]{1,0:T(8,128)}, f32[32,12288]{1,0:T(8,128)}, f32[128,1024]{1,0:T(8,128)}, f32[104,128]{1,0:T(8...) custom-call(bf16[256,1024]{1,0:T(8,128)(2,1)} %bitcast.11, ...), custom_call_target="tpu_custom_call" | custom-call | tf_op jit(solution)/shard_map/pallas_call | solution.py:1352
  297.7 1.2 fusion.2
  298.9 0.0 copy-done.1
  298.9 0.0 copy-done.2
  298.9 0.0 copy-done.3
  298.9 2.0 multiply_subtract_fusion
  300.9 8.2 %shard_map.221 = (f32[32,12288]{1,0:T(8,128)}, f32[32,12288]{1,0:T(8,128)}, f32[32,12288]{1,0:T(8,128)}, f32[128,1024]{1,0:T(8,128)}, f32[128,1024]{1,0:T(8,128)...) custom-call(f32[2,8,128]{2,1,0:T(8,128)} %get-tuple-element.26.norms, ...), custom_call_target="tpu_custom_call" | custom-call | tf_op jit(solution)/shard_map/pallas_call | solution.py:1392
  (2 shorter events, 0.0 us)
Async XLA Ops:
  2.8 0.6 copy-start
  3.4 295.5 %copy-start.1 = (f32[416]{0:T(512)S(1)}, f32[416]{0:T(512)}, u32[]{:S(2)}) copy-start(f32[416]{0:T(512)} %param.23) | copy-start | bytes 4996
  3.4 295.5 %copy-start.2 = (f32[416]{0:T(512)S(1)}, f32[416]{0:T(512)}, u32[]{:S(2)}) copy-start(f32[416]{0:T(512)} %param.24) | copy-start | bytes 4996
  3.4 295.5 %copy-start.3 = (f32[416]{0:T(512)S(1)}, f32[416]{0:T(512)}, u32[]{:S(2)}) copy-start(f32[416]{0:T(512)} %param.25) | copy-start | bytes 4996
